TPU v7x, 32 devices: a whole 2x2x4 slice. The times are simulated.
32 devices in a mesh: band: 8 (over z, y), lon: 4 (over x, core).
Axes of the slice: x: 2, y: 2, z: 4, core: 2. Of those that a mesh axis runs over, the one named last changes fastest.
Arguments:
- jacobian: bfloat16 [65536, 137], P(('band', 'lon')), may hold values from -3 to 3
- departure: float32 [65536], P(('band', 'lon')), may hold values from -6 to 6
- inv_var: float32 [65536], P(('band', 'lon')), may hold values from 0.25 to 4
- frac: float32 [2, 65536], P(None, ('band', 'lon')), may hold values from 0 to 1
- anchors: int32 [2, 65536], P(None, ('band', 'lon')), may hold values from 0 to 511, as said below
- counts: int32 [32, 32], P(('band', 'lon')), may hold values from 0 to 64, as said below
Outputs:
- increments: float32 [137, 256, 512], P(None, 'band', 'lon')
Inputs may be any that keep to these rules, and one draw needn't show every extreme that they name: counts[p, q] is the number of live slots among the 64 that device p holds for owner q; some pairs reach 64 in every draw, and in every draw some owner receives 64 live slots from every device. `anchors`: every slot that device p holds for owner q has its anchor in owner q's block of 32 latitude rows and 128 longitudes, and its latitude row is at most 254.
All inputs are finite; a program needn't handle non-finite values.
Results may differ from a plain program's by a relative error of at most 0.0041.
Values may be sent and summed in bfloat16 or wider, within the bound.
No kernel may reach another device: no remote copies, remote signals or barrier semaphores. Data moves between devices by JAX's collectives and lax.ppermute only.
A program may use at most 64 MiB of HBM per device.

v0:
```python
import math

import jax
import jax.numpy as jnp
from jax import lax
from jax.sharding import PartitionSpec as P

LAT_DEV = 32
LON_DEV = 128


def from_behind(shard, axis, by):
    length = lax.axis_size(axis)
    return lax.ppermute(shard, axis, [(i, (i + by) % length) for i in range(length)])


def shifted(value, axis, steps):
    count = lax.axis_size(axis)
    initial, last = (max(0, -steps), min(count, count - steps))
    return lax.ppermute(value, axis, [(source, source + steps) for source in range(initial, last)])


def block_sums(received, slot_info, first_row, block_rows):
    adjoint_rows = lax.dynamic_slice_in_dim(received, first_row, block_rows, 0)
    row_info = lax.dynamic_slice_in_dim(slot_info, first_row, block_rows, 0)
    lat_local = row_info[:, 4].astype(jnp.int32)
    lon_local = row_info[:, 5].astype(jnp.int32)
    lat_cells = jnp.arange(LAT_DEV + 1, dtype=jnp.int32)
    lon_cells = jnp.arange(LON_DEV, dtype=jnp.int32)
    lat_first = (lat_local[:, None] == lat_cells[None, :]).astype(jnp.bfloat16)
    lat_second = (lat_local[:, None] + 1 == lat_cells[None, :]).astype(jnp.bfloat16)
    lon_first = lon_local[:, None] == lon_cells[None, :]
    lon_second = lon_local[:, None] + 1 == lon_cells[None, :]
    near_row = jnp.where(lon_first, row_info[:, 0:1], 0) + jnp.where(
        lon_second, row_info[:, 1:2], 0
    )
    far_row = jnp.where(lon_first, row_info[:, 2:3], 0) + jnp.where(lon_second, row_info[:, 3:4], 0)
    one_hot = (
        lat_first[:, :, None] * near_row[:, None, :] + lat_second[:, :, None] * far_row[:, None, :]
    )
    one_hot = one_hot.reshape(block_rows, (LAT_DEV + 1) * LON_DEV)
    on_edge = lon_local == LON_DEV - 1
    rim_weight = (
        lat_first * jnp.where(on_edge, row_info[:, 1], 0)[:, None]
        + lat_second * jnp.where(on_edge, row_info[:, 3], 0)[:, None]
    )
    numbers = (((0,), (0,)), ((), ()))
    main_part = lax.dot_general(adjoint_rows, one_hot, numbers, preferred_element_type=jnp.float32)
    rim_part = lax.dot_general(
        adjoint_rows, rim_weight, numbers, preferred_element_type=jnp.float32
    )
    return (main_part, rim_part)


def per_device(jacobian, departure, inv_var, frac, anchors, counts):
    row_total = jacobian.shape[0]
    levels = jacobian.shape[1]
    devices = counts.shape[1]
    capacity = row_total // devices
    lon_count = lax.axis_size("lon")
    within = jnp.arange(capacity, dtype=jnp.int32)
    is_live = (within[None, :] < counts[0][:, None]).reshape(row_total)
    owners = jnp.arange(devices, dtype=jnp.int32)
    lat_start = owners // lon_count * LAT_DEV
    lon_start = owners % lon_count * LON_DEV
    lat_local = (anchors[0].reshape(devices, capacity) - lat_start[:, None]).reshape(row_total)
    lon_local = (anchors[1].reshape(devices, capacity) - lon_start[:, None]).reshape(row_total)
    forcing = departure * inv_var
    adjoint = jnp.where(
        is_live[:, None], forcing[:, None] * jacobian.astype(jnp.float32), 0.0
    ).astype(jnp.bfloat16)
    lat_frac = frac[0]
    lon_frac = frac[1]
    corner_exprs = [
        (1.0 - lat_frac) * (1.0 - lon_frac),
        (1.0 - lat_frac) * lon_frac,
        lat_frac * (1.0 - lon_frac),
        lat_frac * lon_frac,
    ]
    columns = [jnp.where(is_live, value, 0.0) for value in corner_exprs]
    columns = columns + [
        jnp.where(is_live, lat_local, 0).astype(jnp.float32),
        jnp.where(is_live, lon_local, 0).astype(jnp.float32),
    ]
    slot_info = jnp.stack(columns, axis=1).astype(jnp.bfloat16)
    received, row_data = (
        lax.all_to_all(adjoint, ("band", "lon"), split_axis=0, concat_axis=0, tiled=True),
        lax.all_to_all(slot_info, ("band", "lon"), split_axis=0, concat_axis=0, tiled=True),
    )
    block_rows = math.gcd(row_total, 1024)
    main_zero = jnp.zeros((levels, (LAT_DEV + 1) * LON_DEV), jnp.float32)
    rim_zero = jnp.zeros((levels, LAT_DEV + 1), jnp.float32)

    def compute_block(first_row):
        return block_sums(received, row_data, first_row, block_rows)

    def add_block(loop_index, totals):
        first_row = loop_index * block_rows
        main_part, rim_part = compute_block(first_row)
        return (totals[0] + main_part, totals[1] + rim_part)

    main_sum, rim_sum = lax.fori_loop(0, row_total // block_rows, add_block, (main_zero, rim_zero))
    grid_sum = main_sum.reshape(levels, LAT_DEV + 1, LON_DEV)
    from_west = from_behind(rim_sum, "lon", 1)
    grid_sum = grid_sum.at[:, :, 0].add(from_west)
    from_south = shifted(grid_sum[:, LAT_DEV, :], "band", 1)
    return grid_sum[:, :LAT_DEV, :].at[:, 0, :].add(from_south)


def solution(mesh):
    return jax.shard_map(
        per_device,
        mesh=mesh,
        in_specs=(
            P(("band", "lon"), None),
            P(("band", "lon")),
            P(("band", "lon")),
            P(None, ("band", "lon")),
            P(None, ("band", "lon")),
            P(("band", "lon"), None),
        ),
        out_specs=P(None, "band", "lon"),
        check_vma=False,
    )
```

profile of v0, /device:TPU:0, one launch (start us, length us, event | category | flops | bytes accessed | tf_op | source)
XLA Modules:
  0.0 95.2 jit_solution(16440072787862939438)
XLA Ops:
  0.0 0.8 slice_reduce_fusion.3
  0.8 0.1 squeeze.21
  0.9 0.1 squeeze.22
  1.0 0.8 slice_reduce_fusion
  1.8 0.1 reshape_squeeze.7
  1.9 0.1 reshape_squeeze.6
  2.0 0.8 select_convert_fusion.1
  2.8 0.8 convert_convert_fusion
  3.6 0.2 stack.2
  3.8 0.7 reshape.716
  4.5 7.3 %all-to-all-start.1 = ((bf16[32,2,192]{2,1,0:T(2,128)(2,1)}), bf16[32,2,192]{2,1,0:T(2,128)(2,1)S(1)}, u32[]{:S(2)}, u32[]{:S(2)}) async-start(bf16[32,2,192]{2,1,0:T(2,128)(2,1)} %reshape.716), calls=%async_computation.1 | async-start | bytes 65536 | tf_op jit(solution)/shard_map/all_to_all | solution.py:88
  11.8 0.7 iota_compare_fusion.5
  12.5 0.1 lt.89
  12.6 0.7 mul.221
  13.3 1.2 %select_convert_fusion = bf16[2048,137]{0,1:T(8,128)(2,1)S(1)} fusion(bf16[2048,137]{0,1:T(8,128)(2,1)} %param.12, f32[2048]{0:T(1024)S(1)} %mul.221, pred[2048]{0:T(1024)(128)(4,1)S(1)} %lt.89), kind=kLoop, calls=%fused_computation.41 | loop fusion | flops 1122304 | bytes 1132544 | tf_op jit(solution)/shard_map/convert_element_type | solution.py:71
  14.5 1.3 %copy.27 = bf16[2048,137]{1,0:T(8,128)(2,1)} copy(bf16[2048,137]{0,1:T(8,128)(2,1)S(1)} %select_convert_fusion) | data formatting | bytes 1122304 | tf_op jit(solution)/shard_map/all_to_all | solution.py:87
  15.8 3.2 %all-to-all-done.1 = bf16[32,2,192]{2,1,0:T(2,128)(2,1)S(1)} async-done(((bf16[32,2,192]{2,1,0:T(2,128)(2,1)}), bf16[32,2,192]{2,1,0:T(2,128)(2,1)S(1)}, u32[]{:S(2)}, u32[]{:S(2)}) %all-to-all-start.1) | async-done | bytes 24608 | tf_op jit(solution)/shard_map/all_to_all | solution.py:88
  19.0 0.0 copy-start.1
  19.0 2.6 %all-to-all-start = ((bf16[32,64,137]{2,1,0:T(8,128)(2,1)}), bf16[32,64,137]{2,1,0:T(8,128)(2,1)S(1)}, u32[]{:S(2)}, u32[]{:S(2)}) async-start(bf16[32,64,137]{2,1,0:T(8,128)(2,1)} %bitcast.1), calls=%async_computation | async-start | bytes 2097152 | tf_op jit(solution)/shard_map/all_to_all | solution.py:87
  21.7 0.0 copy-done.1
  21.7 0.9 reshape.717
  22.6 0.6 copy.23
  23.2 0.9 all_to_all.18
  24.1 23.8 %all-to-all-done = bf16[32,64,137]{2,1,0:T(8,128)(2,1)S(1)} async-done(((bf16[32,64,137]{2,1,0:T(8,128)(2,1)}), bf16[32,64,137]{2,1,0:T(8,128)(2,1)S(1)}, u32[]{:S(2)}, u32[]{:S(2)}) %all-to-all-start) | async-done | bytes 561184 | tf_op jit(solution)/shard_map/all_to_all | solution.py:87
  47.9 13.1 %while.20 = (s32[]{:T(128)}, f32[137,4224]{1,0:T(8,128)S(1)}, f32[137,33]{0,1:T(8,128)}, bf16[2048,137]{1,0:T(8,128)(2,1)S(1)}, bf16[2048,6]{0,1:T(8,128)(2,1)S(...) while((s32[]{:T(128)}, f32[137,4224]{1,0:T(8,128)S(1)}, ...), condition=%wide.region_1.2_spmd.clone, body=%wide.region_0.1_spmd.clone.sunk | while | flops 1210802304 | bytes 24535148 | solution.py:102
  47.9 0.1 broadcast_add_fusion.5
  48.0 0.1 fusion.39
  48.1 0.8 convolution_add_fusion.5
  49.0 0.2 fusion.40
  49.2 1.2 %multiply_add_fusion.2 = bf16[1024,33,128]{0,2,1:T(8,128)(2,1)S(1)} fusion(bf16[1024,128]{0,1:T(8,128)(2,1)S(1)} %get-tuple-element.286, bf16[1024,33]{0,1:T(8,128)(2,1)S(1)} %get-tuple-element.289, bf16[1024,128]{0,1:T(8,128)(2,1)S(1)} %get-tuple-element.290, bf16[1024,33]{0,1:T(8,128)(2,1)S(1)} %get-tuple-element.291), kind=kLoop, calls=%fused_computation.clone.1 | loop fusion | flops 12976128 | bytes 9310208 | tf_op jit(solution)/shard_map/while/body/eval_jaxpr/add | solution.py:39
  50.4 3.7 %convolution_add_fusion.4 = f32[137,4224]{1,0:T(8,128)S(1)} fusion(bf16[1024,4224]{0,1:T(8,128)(2,1)S(1)} %bitcast.30, f32[137,4224]{1,0:T(8,128)S(1)} %get-tuple-element.309, pred[]{:T(512)S(6)} %compare.20, bf16[2048,137]{1,0:T(8,128)(2,1)S(1)} %get-tuple-element.325, s32[]{:T(128)S(6)} %select_n.237), kind=kOutput, calls=%fused_computation.1.clone.1 | convolution fusion | flops 1186310400 | bytes 13922821 | tf_op jit(solution)/shard_map/while/body/eval_jaxpr/dot_general | solution.py:48
  54.1 0.1 broadcast_add_fusion.5
  54.2 0.1 fusion.39
  54.3 1.6 %convolution_add_fusion.5 = f32[137,33]{0,1:T(8,128)} fusion(bf16[2048,137]{1,0:T(8,128)(2,1)S(1)} %get-tuple-element.325, s32[]{:T(128)S(6)} %select_n.237, s32[1024]{0:T(1024)S(1)} %bitcast.34, s32[1024]{0:T(1024)S(1)} %bitcast.36, f32[137,33]{0,1:T(8,128)} %get-tuple-element.310, bf16[1024]{0:T(1024)(128)(2,1)S(1)} %get-tuple-element.292, ...), kind=kOutput, calls=%fused_computation.2.clone.1 | convolution fusion | flops 9538386 | bytes 572749 | tf_op jit(solution)/shard_map/while/body/eval_jaxpr/dot_general | solution.py:49
  56.0 0.2 fusion.40
  56.1 1.2 %multiply_add_fusion.2 = bf16[1024,33,128]{0,2,1:T(8,128)(2,1)S(1)} fusion(bf16[1024,128]{0,1:T(8,128)(2,1)S(1)} %get-tuple-element.286, bf16[1024,33]{0,1:T(8,128)(2,1)S(1)} %get-tuple-element.289, bf16[1024,128]{0,1:T(8,128)(2,1)S(1)} %get-tuple-element.290, bf16[1024,33]{0,1:T(8,128)(2,1)S(1)} %get-tuple-element.291), kind=kLoop, calls=%fused_computation.clone.1 | loop fusion | flops 12976128 | bytes 9310208 | tf_op jit(solution)/shard_map/while/body/eval_jaxpr/add | solution.py:39
  57.3 3.7 %convolution_add_fusion.4 = f32[137,4224]{1,0:T(8,128)S(1)} fusion(bf16[1024,4224]{0,1:T(8,128)(2,1)S(1)} %bitcast.30, f32[137,4224]{1,0:T(8,128)S(1)} %get-tuple-element.309, pred[]{:T(512)S(6)} %compare.20, bf16[2048,137]{1,0:T(8,128)(2,1)S(1)} %get-tuple-element.325, s32[]{:T(128)S(6)} %select_n.237), kind=kOutput, calls=%fused_computation.1.clone.1 | convolution fusion | flops 1186310400 | bytes 13922821 | tf_op jit(solution)/shard_map/while/body/eval_jaxpr/dot_general | solution.py:48
  61.0 0.1 collective-permute-start
  61.1 1.9 %reshape.683 = f32[137,33,128]{2,1,0:T(8,128)} reshape(f32[137,4224]{1,0:T(8,128)S(1)} %get-tuple-element.162) | data formatting | bytes 4629504 | tf_op jit(solution)/shard_map/reshape | solution.py:103
  63.0 0.0 copy-start
  63.0 1.7 %collective-permute-done = f32[137,33]{0,1:T(8,128)S(1)} collective-permute-done((f32[137,33]{0,1:T(8,128)}, f32[137,33]{0,1:T(8,128)S(1)}, u32[]{:S(2)}, u32[]{:S(2)}) %collective-permute-start) | collective-permute-done | bytes 18116 | tf_op jit(solution)/shard_map/ppermute | solution.py:14
  64.7 3.1 %copy.25 = f32[137,33,1]{2,1,0:T(8,128)} copy(f32[137,33,1]{0,1,2:T(8,128)S(1)} %bitcast.42) | data formatting | bytes 36168 | tf_op jit(solution)/shard_map/reshape.45
  67.8 0.0 copy-done
  67.8 3.7 %slice_add_fusion = f32[137,33,1]{2,1,0:T(8,128)} fusion(f32[137,33,1]{2,1,0:T(8,128)} %copy.25, f32[137,33,128]{2,1,0:T(8,128)S(1)} %copy-done), kind=kLoop, calls=%fused_computation.40 | loop fusion | flops 4521 | bytes 54252 | tf_op jit(solution)/shard_map/add | solution.py:105
  71.5 14.7 %scatter-add.6 = f32[137,33,128]{2,1,0:T(8,128)S(1)} dynamic-update-slice(f32[137,33,128]{2,1,0:T(8,128)S(1)} %copy-done, f32[137,33,1]{2,1,0:T(8,128)} %slice_add_fusion, s32[]{:T(128)} %constant.147.clone.1, s32[]{:T(128)} %constant.147.clone.1, s32[]{:T(128)} %constant.147.clone.1) | dynamic-update-slice | bytes 36172 | tf_op jit(solution)/shard_map/scatter-add | solution.py:105
  86.2 3.4 %collective-permute-start.1 = (f32[137,128]{1,0:T(8,128)S(1)}, f32[137,128]{1,0:T(8,128)S(1)}, u32[]{:S(2)}, u32[]{:S(2)}) collective-permute-start(f32[137,128]{1,0:T(8,128)S(1)} %bitcast.41), channel_id=1, source_target_pairs={{0,4},{4,8},{8,12},{12,16},{16,20},{20,24},{24,28},{1,5},{5,9},{9,... | collective-permute-start | bytes 210440 | tf_op jit(solution)/shard_map/ppermute | solution.py:20
  89.6 1.7 %slice.140 = f32[137,32,128]{2,1,0:T(8,128)} slice(f32[137,33,128]{2,1,0:T(8,128)S(1)} %scatter-add.6), slice={[0:137], [0:32], [0:128]} | slice | bytes 4489216 | tf_op jit(solution)/shard_map/slice | solution.py:107
  91.3 0.3 collective-permute-done.1
  91.6 0.1 slice_add_fusion.1
  91.7 3.5 %scatter-add.9 = f32[137,32,128]{2,1,0:T(8,128)} dynamic-update-slice(f32[137,32,128]{2,1,0:T(8,128)} %slice.140, f32[137,1,128]{2,1,0:T(1,128)S(1)} %slice_add_fusion.1, s32[]{:T(128)} %constant.147.clone.1, s32[]{:T(128)} %constant.147.clone.1, s32[]{:T(128)} %constant.147.clone.1) | dynamic-update-slice | bytes 140292 | tf_op jit(solution)/shard_map/scatter-add | solution.py:107
  (9 shorter events, 0.1 us)
Async XLA Ops:
  4.5 14.6 %all-to-all-start.1 = ((bf16[32,2,192]{2,1,0:T(2,128)(2,1)}), bf16[32,2,192]{2,1,0:T(2,128)(2,1)S(1)}, u32[]{:S(2)}, u32[]{:S(2)}) async-start(bf16[32,2,192]{2,1,0:T(2,128)(2,1)} %reshape.716), calls=%async_computation.1 | async-start | bytes 65536 | tf_op jit(solution)/shard_map/all_to_all | solution.py:88
  19.0 2.7 %copy-start.1 = (bf16[32,2,192]{2,1,0:T(2,128)(2,1)}, bf16[32,2,192]{2,1,0:T(2,128)(2,1)S(1)}, u32[]{:S(2)}) copy-start(bf16[32,2,192]{2,1,0:T(2,128)(2,1)S(1)} %all-to-all-done.1) | copy-start | bytes 73732
  19.0 28.9 %all-to-all-start = ((bf16[32,64,137]{2,1,0:T(8,128)(2,1)}), bf16[32,64,137]{2,1,0:T(8,128)(2,1)S(1)}, u32[]{:S(2)}, u32[]{:S(2)}) async-start(bf16[32,64,137]{2,1,0:T(8,128)(2,1)} %bitcast.1), calls=%async_computation | async-start | bytes 2097152 | tf_op jit(solution)/shard_map/all_to_all | solution.py:87
  61.0 3.7 %collective-permute-start = (f32[137,33]{0,1:T(8,128)}, f32[137,33]{0,1:T(8,128)S(1)}, u32[]{:S(2)}, u32[]{:S(2)}) collective-permute-start(f32[137,33]{0,1:T(8,128)} %get-tuple-element.163), channel_id=1, source_target_pairs={{0,1},{1,2},{2,3},{3,0},{4,5},{5,6},{6,7},{7,4},{8,9},{9,10},{10,1... | collective-permute-start | bytes 54260 | tf_op jit(solution)/shard_map/ppermute | solution.py:14
  63.0 4.8 %copy-start = (f32[137,33,128]{2,1,0:T(8,128)S(1)}, f32[137,33,128]{2,1,0:T(8,128)}, u32[]{:S(2)}) copy-start(f32[137,33,128]{2,1,0:T(8,128)} %reshape.683) | copy-start | bytes 6944260
  86.2 5.4 %collective-permute-start.1 = (f32[137,128]{1,0:T(8,128)S(1)}, f32[137,128]{1,0:T(8,128)S(1)}, u32[]{:S(2)}, u32[]{:S(2)}) collective-permute-start(f32[137,128]{1,0:T(8,128)S(1)} %bitcast.41), channel_id=1, source_target_pairs={{0,4},{4,8},{8,12},{12,16},{16,20},{20,24},{24,28},{1,5},{5,9},{9,... | collective-permute-start | bytes 210440 | tf_op jit(solution)/shard_map/ppermute | solution.py:20
where the time goes:
time: 96 us; the launch traced here: 95.2 us
  local copies, waits for them, and re-layouts  31.5 us (33%)
  waiting for transfers between devices  29 us (30%)
  starting transfers between devices  13.4 us (14%)
  other arithmetic  11.2 us (12%)
  matrix products  9.77 us (10%)
    all_to_all x1, waiting for transfers between devices, per_device(): lax.all_to_all(adjoint, ('band', 'lon'), split_axis=0, concat_axis=0, til...  23.8 us
    scatter-add x1, local copies, waits for them, and re-layouts, per_device(): grid_sum = grid_sum.at[:, :, 0].add(from_west)  14.7 us
    dot_general x2, matrix products, block_sums(): lax.dot_general(adjoint_rows, one_hot, numbers, preferred_element_type=jn...  7.34 us
    all_to_all x1, starting transfers between devices, per_device(): lax.all_to_all(slot_info, ('band', 'lon'), split_axis=0, concat_axis=0, t...  7.3 us
    add x1, other arithmetic, per_device(): grid_sum = grid_sum.at[:, :, 0].add(from_west)  3.67 us
    scatter-add x1, local copies, waits for them, and re-layouts, per_device(): return grid_sum[:, :LAT_DEV, :].at[:, 0, :].add(from_south)  3.48 us
    ppermute x1, starting transfers between devices, shifted(): lax.ppermute(value, axis, [(source, source + steps) for source in range(i...  3.4 us
    all_to_all x1, waiting for transfers between devices, per_device(): lax.all_to_all(slot_info, ('band', 'lon'), split_axis=0, concat_axis=0, t...  3.21 us
  transfers between devices with their start and end apart: 4, of which 4 were waited for; matrix products, arithmetic and copies ran while one was open for 10% of the time, Pallas kernels for 0%

commit v1 on v0

v1 whole, which is shorter than its diff:
```python
import functools

import jax
import jax.numpy as jnp
from jax import lax
from jax.experimental import pallas as pl
from jax.experimental.pallas import tpu as pltpu
from jax.sharding import PartitionSpec as P

LAT_DEV = 32
LON_DEV = 128
LANES = 128
N_INFO = 6
F32 = jnp.float32
BF16 = jnp.bfloat16
NT = (((1,), (1,)), ((), ()))
VMEM_LIMIT = 48 * 1024 * 1024


def lane_iota(shape):
    return lax.broadcasted_iota(jnp.int32, shape, len(shape) - 1)


def row_iota(shape):
    return lax.broadcasted_iota(jnp.int32, shape, 0)


def swap_halves(first, second, cap):
    low = lane_iota(first.shape) < cap
    return (
        jnp.where(low, first, pltpu.roll(second, cap, 1)),
        jnp.where(low, pltpu.roll(first, cap, 1), second),
    )


def pack_kernel(counts_ref, jac_ref, dep_ref, inv_ref, frac_ref, anchor_ref, out_ref, *, cap, lon_count):
    levels, slots = jac_ref.shape
    half = out_ref.shape[1]
    body = (levels // 8) * 8
    rest = levels - body
    lane = lane_iota((1, LANES))
    low = lane < cap
    for tile in range(slots // LANES):
        at = pl.ds(tile * LANES, LANES)
        first, second = 2 * tile, 2 * tile + 1
        count = jnp.where(low, counts_ref[0, first], counts_ref[0, second] + cap)
        live = lane < count
        forcing = jnp.where(live, dep_ref[:, at] * inv_ref[:, at], 0.0)
        a = frac_ref[0:1, at]
        b = frac_ref[1:2, at]
        lat0 = jnp.where(low, first // lon_count * LAT_DEV, second // lon_count * LAT_DEV)
        lon0 = jnp.where(low, first % lon_count * LON_DEV, second % lon_count * LON_DEV)
        info = [
            (1.0 - a) * (1.0 - b),
            (1.0 - a) * b,
            a * (1.0 - b),
            a * b,
            (anchor_ref[0:1, at] - lat0).astype(F32),
            (anchor_ref[1:2, at] - lon0).astype(F32),
        ]
        adjoint = jac_ref[0:body, at].astype(F32) * forcing
        tail_rows = 2 * half - body
        tail = jnp.zeros((tail_rows, LANES), F32)
        row = row_iota((tail_rows, LANES))
        for i in range(rest):
            tail = jnp.where(row == i, jac_ref[body + i : body + i + 1, at].astype(F32) * forcing, tail)
        for i, value in enumerate(info):
            tail = jnp.where(row == rest + i, jnp.where(live, value, 0.0), tail)
        whole = jnp.concatenate([adjoint, tail], axis=0)
        one, two = swap_halves(whole[:half], whole[half:], cap)
        out_ref[first] = one.astype(BF16)
        out_ref[second] = two.astype(BF16)


def rim_kernel(recv_ref, x_ref, info_ref, east_ref, north_ref, hot_ref, *, cap, levels):
    devices, half, _ = recv_ref.shape
    body = (levels // 8) * 8
    rest = levels - body
    row = row_iota((LON_DEV, LANES)).astype(F32)
    for tile in range(devices // 2):
        at = pl.ds(tile * LANES, LANES)
        low, high = swap_halves(recv_ref[2 * tile].astype(F32), recv_ref[2 * tile + 1].astype(F32), cap)
        whole = jnp.concatenate([low, high], axis=0)
        x_ref[:, at] = whole.astype(BF16)
        info = whole[body:]
        info_ref[:, at] = info
        w01, w10, w11, lat, lon = [info[rest + i : rest + i + 1] for i in range(1, N_INFO)]
        top = lat == LAT_DEV - 1.0
        w10 = jnp.where(top, w10, 0.0)
        w11_top = jnp.where(top, w11, 0.0)
        hot_ref[0:LON_DEV, at] = jnp.where(
            row == lon, w10, jnp.where(row == lon + 1.0, w11_top, 0.0)
        ).astype(BF16)
        edge = lon == LON_DEV - 1.0
        w01 = jnp.where(edge, w01, 0.0)
        w11 = jnp.where(edge, w11, 0.0)
        hot_ref[LON_DEV:, at] = jnp.where(
            row == lat, w01, jnp.where(row == lat + 1.0, w11, 0.0)
        ).astype(BF16)
    sums = lax.dot_general(x_ref[...], hot_ref[...], NT, preferred_element_type=F32)
    north_ref[...] = sums[:, :LON_DEV]
    east_ref[...] = sums[:, LON_DEV:]


def main_kernel(x_ref, info_ref, out_ref, near_ref, far_ref, lat_ref, *, levels):
    slots = x_ref.shape[1]
    rest = levels % 8
    row = row_iota((LON_DEV, LANES)).astype(F32)
    for tile in range(slots // LANES):
        at = pl.ds(tile * LANES, LANES)
        w00, w01, w10, w11, lat, lon = [info_ref[rest + i : rest + i + 1, at] for i in range(N_INFO)]
        here = row == lon
        after = row == lon + 1.0
        near_ref[:, at] = jnp.where(here, w00, jnp.where(after, w01, 0.0)).astype(BF16)
        far_ref[:, at] = jnp.where(here, w10, jnp.where(after, w11, 0.0)).astype(BF16)
        lat_ref[:, at] = jnp.broadcast_to(lat, (LON_DEV, LANES)).astype(BF16)

    def two_rows(step, carry):
        lat = lat_ref[...]
        near = near_ref[...]
        far = far_ref[...]
        zero = jnp.zeros_like(near)
        hots = []
        for i in range(2):
            r = (2 * step + i).astype(F32).astype(BF16)
            before = (2 * step + i - 1).astype(F32).astype(BF16)
            hots.append(jnp.where(lat == r, near, jnp.where(lat == before, far, zero)))
        hot = jnp.concatenate(hots, axis=0)
        sums = lax.dot_general(x_ref[...], hot, NT, preferred_element_type=F32)
        out_ref[2 * step] = sums[:, :LON_DEV]
        out_ref[2 * step + 1] = sums[:, LON_DEV:]
        return carry

    lax.fori_loop(0, LAT_DEV // 2, two_rows, 0)


def final_kernel(acc_ref, east_ref, north_ref, corner_ref, out_ref):
    rows = acc_ref.shape[1]
    lane = lane_iota((rows, LANES))
    first = lane == 0
    east = east_ref[...]
    for r in range(LAT_DEV):
        value = acc_ref[r] + jnp.where(first, east if r == 0 else pltpu.roll(east, LANES - r, 1), 0.0)
        if r == 0:
            value = value + north_ref[...]
            value = value + jnp.where(first, pltpu.roll(corner_ref[...], LANES - LAT_DEV, 1), 0.0)
        out_ref[pl.ds(r, rows, LAT_DEV), :] = value


def per_device(jacobian, departure, inv_var, frac, anchors, counts, *, n_band, n_lon):
    slots, levels = jacobian.shape
    devices = counts.shape[1]
    cap = slots // devices
    rows = -(-(levels + N_INFO) // 16) * 16
    half = rows // 2
    vmem = pl.BlockSpec(memory_space=pltpu.VMEM)
    smem = pl.BlockSpec(memory_space=pltpu.SMEM)
    params = pltpu.CompilerParams(vmem_limit_bytes=VMEM_LIMIT)
    struct = jax.ShapeDtypeStruct

    payload = pl.pallas_call(
        functools.partial(pack_kernel, cap=cap, lon_count=n_lon),
        out_shape=struct((devices, half, LANES), BF16),
        in_specs=[smem] + [vmem] * 5,
        out_specs=vmem,
        compiler_params=params,
        name="pack",
    )(counts, jacobian.T, departure[None, :], inv_var[None, :], frac, anchors)

    received = lax.all_to_all(payload, ("band", "lon"), split_axis=0, concat_axis=0, tiled=True)

    tail_rows = rows - levels // 8 * 8
    x, info, east, north = pl.pallas_call(
        functools.partial(rim_kernel, cap=cap, levels=levels),
        out_shape=(
            struct((rows, slots), BF16),
            struct((tail_rows, slots), F32),
            struct((rows, LANES), F32),
            struct((rows, LANES), F32),
        ),
        in_specs=[vmem],
        out_specs=(vmem,) * 4,
        scratch_shapes=[pltpu.VMEM((2 * LANES, slots), BF16)],
        compiler_params=params,
        name="rim",
    )(received)

    def place(band, lon):
        return band * n_lon + lon % n_lon

    corner_pairs = [
        (place(i, j), place(i + 1, j + 1)) for i in range(n_band - 1) for j in range(n_lon)
    ]
    corner_in = lax.ppermute(east, ("band", "lon"), corner_pairs)
    east_in = lax.ppermute(east, "lon", [(j, (j + 1) % n_lon) for j in range(n_lon)])
    north_in = lax.ppermute(north, "band", [(i, i + 1) for i in range(n_band - 1)])

    acc = pl.pallas_call(
        functools.partial(main_kernel, levels=levels),
        out_shape=struct((LAT_DEV, rows, LANES), F32),
        in_specs=[vmem] * 2,
        out_specs=vmem,
        scratch_shapes=[pltpu.VMEM((LON_DEV, slots), BF16)] * 3,
        compiler_params=params,
        cost_estimate=pl.CostEstimate(
            flops=2 * rows * slots * LAT_DEV * LON_DEV, bytes_accessed=4 * LAT_DEV * rows * LANES, transcendentals=0
        ),
        name="main",
    )(x, info)

    block = rows // 3
    out = pl.pallas_call(
        final_kernel,
        grid=(3,),
        out_shape=struct((levels * LAT_DEV, LON_DEV), F32),
        in_specs=[pl.BlockSpec((LAT_DEV, block, LANES), lambda i: (0, i, 0))]
        + [pl.BlockSpec((block, LANES), lambda i: (i, 0))] * 3,
        out_specs=pl.BlockSpec((block * LAT_DEV, LON_DEV), lambda i: (i, 0)),
        compiler_params=params,
        name="final",
    )(acc, east_in, north_in, corner_in)
    return out.reshape(levels, LAT_DEV, LON_DEV)


def solution(mesh):
    both = ("band", "lon")
    return jax.shard_map(
        functools.partial(per_device, n_band=mesh.shape["band"], n_lon=mesh.shape["lon"]),
        mesh=mesh,
        in_specs=(P(both, None), P(both), P(both), P(None, both), P(None, both), P(both, None)),
        out_specs=P(None, "band", "lon"),
        check_vma=False,
    )
```

time: 96 us -> 52.1 us (0.54)
  waiting for transfers between devices: 29 us -> 0.01 us
  local copies, waits for them, and re-layouts: 31.5 us -> 4.54 us
  blocking collectives: 0 us -> 23.8 us
  Pallas kernels: 0 us -> 16.5 us
  other arithmetic: 11.2 us -> 0 us
  matrix products: 9.77 us -> 0 us
  starting transfers between devices: 13.4 us -> 6.61 us
    all_to_all x2 -> x0, waiting for transfers between devices: 27 us -> none  [the longest x1 23.8 us: per_device(): lax.all_to_all(adjoint, ('band', 'lon'), split_axis=0, concat_axis=0, til...]
    all_to_all x0 -> x1, blocking collectives: none -> 23.8 us  [per_device(): lax.all_to_all(payload, ('band', 'lon'), split_axis=0, concat_axis=0, til...]
    scatter-add x2 -> x0, local copies, waits for them, and re-layouts: 18.2 us -> none  [the longest x1 14.7 us: per_device(): grid_sum = grid_sum.at[:, :, 0].add(from_west)]
    pallas_call x0 -> x4, Pallas kernels: none -> 16.5 us  [the longest x1 10.9 us: per_device(): pl.pallas_call(functools.partial(main_kernel, levels=levels), out_shape=s...]
    all_to_all x2 -> x0, starting transfers between devices: 9.94 us -> none  [the longest x1 7.3 us: per_device(): lax.all_to_all(slot_info, ('band', 'lon'), split_axis=0, concat_axis=0, t...]
    dot_general x4 -> x0, matrix products: 9.77 us -> none  [the longest x2 7.34 us: block_sums(): lax.dot_general(adjoint_rows, one_hot, numbers, preferred_element_type=jn...]
    add x10 -> x0, other arithmetic: 6.63 us -> none  [the longest x1 3.67 us: per_device(): grid_sum = grid_sum.at[:, :, 0].add(from_west)]
    another operation x4 -> x0, local copies, waits for them, and re-layouts: 3.42 us -> none
  transfers between devices with their start and end apart: 4 -> 3, of which waited for: 4 -> 0; matrix products, arithmetic and copies ran while one was open for 10% -> 0% of each run, Pallas kernels for 0% -> 21%
where the time goes in v1:
time: 52.1 us; the launch traced here: 51.6 us
  blocking collectives  23.8 us (46%)
  Pallas kernels  16.5 us (32%)
  starting transfers between devices  6.61 us (13%)
  local copies, waits for them, and re-layouts  4.54 us (9%)
    all_to_all x1, blocking collectives, per_device(): lax.all_to_all(payload, ('band', 'lon'), split_axis=0, concat_axis=0, til...  23.8 us
    pallas_call x1, Pallas kernels, per_device(): pl.pallas_call(functools.partial(main_kernel, levels=levels), out_shape=s...  10.9 us
    unnamed x12, local copies, waits for them, and re-layouts  4.54 us
    pallas_call x1, Pallas kernels, per_device(): pl.pallas_call(final_kernel, grid=(3,), out_shape=struct((levels * LAT_DE...  3.71 us
    ppermute x1, starting transfers between devices, per_device(): corner_in = lax.ppermute(east, ('band', 'lon'), corner_pairs)  2.57 us
    ppermute x1, starting transfers between devices, per_device(): lax.ppermute(north, 'band', [(i, i + 1) for i in range(n_band - 1)])  2.47 us
    ppermute x1, starting transfers between devices, per_device(): lax.ppermute(east, 'lon', [(j, (j + 1) % n_lon) for j in range(n_lon)])  1.57 us
  transfers between devices with their start and end apart: 3, of which 0 were waited for; matrix products, arithmetic and copies ran while one was open for 0% of the time, Pallas kernels for 21%

profile of v1, /device:TPU:0, one launch (start us, length us, event | category | flops | bytes accessed | tf_op | source)
XLA Modules:
  0.0 51.6 jit_solution(8024588506406434487)
XLA Ops:
  0.0 0.0 copy-start
  0.0 1.1 %copy-done = bf16[2048,137]{0,1:T(8,128)(2,1)S(1)} copy-done((bf16[2048,137]{0,1:T(8,128)(2,1)S(1)}, bf16[2048,137]{0,1:T(8,128)(2,1)}, u32[]{:S(2)}) %copy-start) | copy-done | bytes 561176
  1.1 0.0 copy-start.1
  1.1 0.7 %copy-done.1 = f32[2,2048]{1,0:T(2,128)S(1)} copy-done((f32[2,2048]{1,0:T(2,128)S(1)}, f32[2,2048]{1,0:T(2,128)}, u32[]{:S(2)}) %copy-start.1) | copy-done | bytes 16408
  1.8 0.0 copy-start.2
  1.8 0.7 %copy-done.2 = s32[2,2048]{1,0:T(2,128)S(1)} copy-done((s32[2,2048]{1,0:T(2,128)S(1)}, s32[2,2048]{1,0:T(2,128)}, u32[]{:S(2)}) %copy-start.2) | copy-done | bytes 16408
  2.5 0.0 copy-start.3
  2.5 0.7 %copy-done.3 = f32[2048]{0:T(1024)S(1)} copy-done((f32[2048]{0:T(1024)S(1)}, f32[2048]{0:T(1024)}, u32[]{:S(2)}) %copy-start.3) | copy-done | bytes 8216
  3.2 0.0 copy-start.4
  3.2 0.7 %copy-done.4 = f32[2048]{0:T(1024)S(1)} copy-done((f32[2048]{0:T(1024)S(1)}, f32[2048]{0:T(1024)}, u32[]{:S(2)}) %copy-start.4) | copy-done | bytes 8216
  3.9 0.0 copy-start.5
  3.9 0.7 %copy-done.5 = s32[1,32]{1,0:T(1,128)S(1)} copy-done((s32[1,32]{1,0:T(1,128)S(1)}, s32[1,32]{1,0:T(1,128)}, u32[]{:S(2)}) %copy-start.5) | copy-done | bytes 152
  4.6 0.9 %pack.1 = bf16[32,72,128]{2,1,0:T(8,128)(2,1)S(1)} custom-call(s32[1,32]{1,0:T(1,128)S(1)} %copy-done.5, bf16[137,2048]{1,0:T(8,128)(2,1)S(1)} %bitcast.4, f32[1,2048]{1,0:T(1,128)S(1)} %bitcast.5, f32[1,2048]{1,0:T(1,128)S(1)} %bitcast.6, f32[2,2048]{1,0:T(2,128)S(1)} %copy-done.1, s32[2,2048]{1,0:T(2,128)S(1)} %copy-done.2), custom_call_target="tpu_custom_call" | custom-call | tf_op jit(solution)/shard_map/pack/pallas_call | solution.py:161
  5.4 23.8 %all_to_all.5.recv_ref = bf16[32,72,128]{2,1,0:T(8,128)(2,1)S(1)} all-to-all(bf16[32,72,128]{2,1,0:T(8,128)(2,1)S(1)} %pack.1), channel_id=1, replica_groups=mesh['band'=8,'lon'=4] {'band','lon'}, dimensions={0} | all-to-all | bytes 1179648 | tf_op jit(solution)/shard_map/all_to_all | solution.py:170
  29.2 1.0 %rim.1 = (bf16[144,2048]{1,0:T(8,128)(2,1)S(1)}, f32[8,2048]{1,0:T(8,128)S(1)}, f32[144,128]{1,0:T(8,128)S(1)}, f32[144,128]{1,0:T(8,128)S(1)}) custom-call(bf16[32,72,128]{2,1,0:T(8,128)(2,1)S(1)} %all_to_all.5.recv_ref), custom_call_target="tpu_custom_call" | custom-call | tf_op jit(solution)/shard_map/rim/pallas_call | solution.py:173
  30.3 2.6 %collective-permute-start.2 = (f32[144,128]{1,0:T(8,128)S(1)}, f32[144,128]{1,0:T(8,128)S(1)}, u32[]{:S(2)}, u32[]{:S(2)}) collective-permute-start(f32[144,128]{1,0:T(8,128)S(1)} %get-tuple-element.11), channel_id=1, source_target_pairs={{0,5},{1,6},{2,7},{3,4},{4,9},{5,10},{6,11},{7,8},{8,13},{9,14},{1... | collective-permute-start | bytes 221192 | tf_op jit(solution)/shard_map/ppermute | solution.py:194
  32.9 1.6 %collective-permute-start = (f32[144,128]{1,0:T(8,128)S(1)}, f32[144,128]{1,0:T(8,128)S(1)}, u32[]{:S(2)}, u32[]{:S(2)}) collective-permute-start(f32[144,128]{1,0:T(8,128)S(1)} %get-tuple-element.11), channel_id=1, source_target_pairs={{0,1},{1,2},{2,3},{3,0},{4,5},{5,6},{6,7},{7,4},{8,9},{9,10},{10,1... | collective-permute-start | bytes 221192 | tf_op jit(solution)/shard_map/ppermute | solution.py:195
  34.4 2.5 %collective-permute-start.1 = (f32[144,128]{1,0:T(8,128)S(1)}, f32[144,128]{1,0:T(8,128)S(1)}, u32[]{:S(2)}, u32[]{:S(2)}) collective-permute-start(f32[144,128]{1,0:T(8,128)S(1)} %get-tuple-element.12), channel_id=1, source_target_pairs={{0,4},{4,8},{8,12},{12,16},{16,20},{20,24},{24,28},{1,5},{5,9},{9,... | collective-permute-start | bytes 221192 | tf_op jit(solution)/shard_map/ppermute | solution.py:196
  36.9 10.9 %main.1.acc_ref = f32[32,144,128]{2,1,0:T(8,128)S(1)} custom-call(bf16[144,2048]{1,0:T(8,128)(2,1)S(1)} %get-tuple-element.9.x_ref, f32[8,2048]{1,0:T(8,128)S(1)} %get-tuple-element.10.info_ref), custom_call_target="tpu_custom_call" | custom-call | flops 2415919104 | bytes 2359296 | tf_op jit(solution)/shard_map/main/pallas_call | solution.py:198
  47.9 0.0 collective-permute-done.1.north_ref
  47.9 0.0 collective-permute-done.2.corner_ref
  47.9 0.0 collective-permute-done.east_ref
  47.9 3.7 %final.1 = f32[4384,128]{1,0:T(8,128)} custom-call(f32[32,144,128]{2,1,0:T(8,128)S(1)} %main.1.acc_ref, f32[144,128]{1,0:T(8,128)S(1)} %collective-permute-done.east_ref, f32[144,128]{1,0:T(8,128)S(1)} %collective-permute-done.1.north_ref, f32[144,128]{1,0:T(8,128)S(1)} %collective-permute-done.2.corner_ref), custom_call_target="tpu_custom_call" | custom-call | tf_op jit(solution)/shard_map/final/pallas_call | solution.py:212
Async XLA Ops:
  0.0 1.1 %copy-start = (bf16[2048,137]{0,1:T(8,128)(2,1)S(1)}, bf16[2048,137]{0,1:T(8,128)(2,1)}, u32[]{:S(2)}) copy-start(bf16[2048,137]{0,1:T(8,128)(2,1)} %param.6) | copy-start | bytes 1683460
  1.1 0.7 %copy-start.1 = (f32[2,2048]{1,0:T(2,128)S(1)}, f32[2,2048]{1,0:T(2,128)}, u32[]{:S(2)}) copy-start(f32[2,2048]{1,0:T(2,128)} %frac_ref.1) | copy-start | bytes 49156
  1.8 0.7 %copy-start.2 = (s32[2,2048]{1,0:T(2,128)S(1)}, s32[2,2048]{1,0:T(2,128)}, u32[]{:S(2)}) copy-start(s32[2,2048]{1,0:T(2,128)} %anchor_ref.1) | copy-start | bytes 49156
  2.5 0.7 %copy-start.3 = (f32[2048]{0:T(1024)S(1)}, f32[2048]{0:T(1024)}, u32[]{:S(2)}) copy-start(f32[2048]{0:T(1024)} %param.7) | copy-start | bytes 24580
  3.2 0.7 %copy-start.4 = (f32[2048]{0:T(1024)S(1)}, f32[2048]{0:T(1024)}, u32[]{:S(2)}) copy-start(f32[2048]{0:T(1024)} %param.8) | copy-start | bytes 24580
  3.9 0.7 %copy-start.5 = (s32[1,32]{1,0:T(1,128)S(1)}, s32[1,32]{1,0:T(1,128)}, u32[]{:S(2)}) copy-start(s32[1,32]{1,0:T(1,128)} %counts_ref.1) | copy-start | bytes 388
  30.3 17.6 %collective-permute-start.2 = (f32[144,128]{1,0:T(8,128)S(1)}, f32[144,128]{1,0:T(8,128)S(1)}, u32[]{:S(2)}, u32[]{:S(2)}) collective-permute-start(f32[144,128]{1,0:T(8,128)S(1)} %get-tuple-element.11), channel_id=1, source_target_pairs={{0,5},{1,6},{2,7},{3,4},{4,9},{5,10},{6,11},{7,8},{8,13},{9,14},{1... | collective-permute-start | bytes 221192 | tf_op jit(solution)/shard_map/ppermute | solution.py:194
  32.9 15.0 %collective-permute-start = (f32[144,128]{1,0:T(8,128)S(1)}, f32[144,128]{1,0:T(8,128)S(1)}, u32[]{:S(2)}, u32[]{:S(2)}) collective-permute-start(f32[144,128]{1,0:T(8,128)S(1)} %get-tuple-element.11), channel_id=1, source_target_pairs={{0,1},{1,2},{2,3},{3,0},{4,5},{5,6},{6,7},{7,4},{8,9},{9,10},{10,1... | collective-permute-start | bytes 221192 | tf_op jit(solution)/shard_map/ppermute | solution.py:195
  34.4 13.4 %collective-permute-start.1 = (f32[144,128]{1,0:T(8,128)S(1)}, f32[144,128]{1,0:T(8,128)S(1)}, u32[]{:S(2)}, u32[]{:S(2)}) collective-permute-start(f32[144,128]{1,0:T(8,128)S(1)} %get-tuple-element.12), channel_id=1, source_target_pairs={{0,4},{4,8},{8,12},{12,16},{16,20},{20,24},{24,28},{1,5},{5,9},{9,... | collective-permute-start | bytes 221192 | tf_op jit(solution)/shard_map/ppermute | solution.py:196

commit v2 on v1

--- a/solution.py
+++ b/solution.py
@@ -15,6 +15,14 @@
 BF16 = jnp.bfloat16
 NT = (((1,), (1,)), ((), ()))
 VMEM_LIMIT = 48 * 1024 * 1024
+VMEM_ALL = 64 * 1024 * 1024
+SPAN = 8
+STEP_LEVELS = 16
+JAC_CHUNKS = 4
+
+
+def bf(value):
+    return jnp.asarray(value, F32).astype(BF16)
 
 
 def lane_iota(shape):
@@ -33,14 +41,45 @@
     )
 
 
-def pack_kernel(counts_ref, jac_ref, dep_ref, inv_ref, frac_ref, anchor_ref, out_ref, *, cap, lon_count):
+def pack_kernel(
+    counts_hbm, jac_hbm, dep_hbm, inv_hbm, frac_hbm, anchor_hbm, out_hbm,
+    out_ref, counts_ref, jac_ref, dep_ref, inv_ref, frac_ref, anchor_ref, sems, *, cap, lon_count,
+):
     levels, slots = jac_ref.shape
     half = out_ref.shape[1]
     body = (levels // 8) * 8
     rest = levels - body
+    small = [
+        pltpu.make_async_copy(src, dst, sems.at[i])
+        for i, (src, dst) in enumerate(
+            [
+                (counts_hbm, counts_ref),
+                (dep_hbm, dep_ref),
+                (inv_hbm, inv_ref),
+                (frac_hbm, frac_ref),
+                (anchor_hbm, anchor_ref),
+            ]
+        )
+    ]
+    chunk = slots // JAC_CHUNKS
+    large = [
+        pltpu.make_async_copy(
+            jac_hbm.at[:, pl.ds(i * chunk, chunk)],
+            jac_ref.at[:, pl.ds(i * chunk, chunk)],
+            sems.at[len(small) + i],
+        )
+        for i in range(JAC_CHUNKS)
+    ]
+    for copy in small + large:
+        copy.start()
+    for copy in small:
+        copy.wait()
+    stores = []
     lane = lane_iota((1, LANES))
     low = lane < cap
     for tile in range(slots // LANES):
+        if tile * LANES % chunk == 0:
+            large[tile * LANES // chunk].wait()
         at = pl.ds(tile * LANES, LANES)
         first, second = 2 * tile, 2 * tile + 1
         count = jnp.where(low, counts_ref[0, first], counts_ref[0, second] + cap)
@@ -70,6 +109,14 @@
         one, two = swap_halves(whole[:half], whole[half:], cap)
         out_ref[first] = one.astype(BF16)
         out_ref[second] = two.astype(BF16)
+        if (tile + 1) * LANES % chunk == 0:
+            done = tile * LANES // chunk
+            part = pl.ds(done * chunk // cap, chunk // cap)
+            copy = pltpu.make_async_copy(out_ref.at[part], out_hbm.at[part], sems.at[len(small) + JAC_CHUNKS + done])
+            copy.start()
+            stores.append(copy)
+    for copy in stores:
+        copy.wait()
 
 
 def rim_kernel(recv_ref, x_ref, info_ref, east_ref, north_ref, hot_ref, *, cap, levels):
@@ -102,49 +149,66 @@
     east_ref[...] = sums[:, LON_DEV:]
 
 
-def main_kernel(x_ref, info_ref, out_ref, near_ref, far_ref, lat_ref, *, levels):
-    slots = x_ref.shape[1]
+def main_kernel(x_ref, info_ref, out_ref, near_ref, far_ref, left_ref, *, levels):
+    rows, slots = x_ref.shape
     rest = levels % 8
     row = row_iota((LON_DEV, LANES)).astype(F32)
     for tile in range(slots // LANES):
         at = pl.ds(tile * LANES, LANES)
-        w00, w01, w10, w11, lat, lon = [info_ref[rest + i : rest + i + 1, at] for i in range(N_INFO)]
+        w00, w01, w10, w11, _, lon = [info_ref[rest + i : rest + i + 1, at] for i in range(N_INFO)]
         here = row == lon
         after = row == lon + 1.0
         near_ref[:, at] = jnp.where(here, w00, jnp.where(after, w01, 0.0)).astype(BF16)
         far_ref[:, at] = jnp.where(here, w10, jnp.where(after, w11, 0.0)).astype(BF16)
-        lat_ref[:, at] = jnp.broadcast_to(lat, (LON_DEV, LANES)).astype(BF16)
-
-    def two_rows(step, carry):
-        lat = lat_ref[...]
-        near = near_ref[...]
-        far = far_ref[...]
-        zero = jnp.zeros_like(near)
+    lat = info_ref[rest + 4 : rest + 5, :]
+    group = jnp.floor(lat * (1.0 / SPAN))
+    within = (lat - group * SPAN).astype(BF16)
+    group = group.astype(BF16)
+    lat = lat.astype(BF16)
+    groups = LAT_DEV // SPAN
+    x = x_ref[...]
+    zero_x = jnp.zeros_like(x)
+    for u in range(groups):
+        left_ref[u * rows : (u + 1) * rows, :] = jnp.where(group == bf(u), x, zero_x)
+    zero = jnp.zeros((LON_DEV, slots), BF16)
+    far = far_ref[...]
+    hot = jnp.concatenate([jnp.where(lat == bf(SPAN * u - 1), far, zero) for u in range(1, groups)], axis=0)
+    seam = lax.dot_general(x, hot, NT, preferred_element_type=F32)
+    for first in range(0, SPAN, 2):
         hots = []
-        for i in range(2):
-            r = (2 * step + i).astype(F32).astype(BF16)
-            before = (2 * step + i - 1).astype(F32).astype(BF16)
-            hots.append(jnp.where(lat == r, near, jnp.where(lat == before, far, zero)))
-        hot = jnp.concatenate(hots, axis=0)
-        sums = lax.dot_general(x_ref[...], hot, NT, preferred_element_type=F32)
-        out_ref[2 * step] = sums[:, :LON_DEV]
-        out_ref[2 * step + 1] = sums[:, LON_DEV:]
-        return carry
-
-    lax.fori_loop(0, LAT_DEV // 2, two_rows, 0)
-
-
-def final_kernel(acc_ref, east_ref, north_ref, corner_ref, out_ref):
+        for v in (first, first + 1):
+            far_part = jnp.where(within == bf(v - 1), far_ref[...], zero) if v else zero
+            hots.append(jnp.where(within == bf(v), near_ref[...], far_part))
+        sums = lax.dot_general(left_ref[...], jnp.concatenate(hots, axis=0), NT, preferred_element_type=F32)
+        for u in range(groups):
+            for v in (first, first + 1):
+                value = sums[u * rows : (u + 1) * rows, (v - first) * LON_DEV : (v - first + 1) * LON_DEV]
+                if v == 0 and u > 0:
+                    value = value + seam[:, (u - 1) * LON_DEV : u * LON_DEV]
+                out_ref[u * SPAN + v] = value
+
+
+def final_kernel(acc_ref, east_ref, north_ref, corner_ref, out_hbm, out_ref, sems, *, levels):
     rows = acc_ref.shape[1]
-    lane = lane_iota((rows, LANES))
+    lane = lane_iota((STEP_LEVELS, LANES))
     first = lane == 0
-    east = east_ref[...]
-    for r in range(LAT_DEV):
-        value = acc_ref[r] + jnp.where(first, east if r == 0 else pltpu.roll(east, LANES - r, 1), 0.0)
-        if r == 0:
-            value = value + north_ref[...]
-            value = value + jnp.where(first, pltpu.roll(corner_ref[...], LANES - LAT_DEV, 1), 0.0)
-        out_ref[pl.ds(r, rows, LAT_DEV), :] = value
+    copies = []
+    for start in range(0, rows, STEP_LEVELS):
+        at = pl.ds(start, STEP_LEVELS)
+        east = east_ref[at, :]
+        for r in range(LAT_DEV):
+            value = acc_ref[r, at, :] + jnp.where(first, pltpu.roll(east, LANES - r, 1) if r else east, 0.0)
+            if r == 0:
+                value = value + north_ref[at, :]
+                value = value + jnp.where(first, pltpu.roll(corner_ref[at, :], LANES - LAT_DEV, 1), 0.0)
+            out_ref[pl.ds(start * LAT_DEV + r, STEP_LEVELS, LAT_DEV), :] = value
+        stop = min(start + STEP_LEVELS, levels)
+        span = pl.ds(start * LAT_DEV, (stop - start) * LAT_DEV)
+        copy = pltpu.make_async_copy(out_ref.at[span, :], out_hbm.at[span, :], sems.at[len(copies)])
+        copy.start()
+        copies.append(copy)
+    for copy in copies:
+        copy.wait()
 
 
 def per_device(jacobian, departure, inv_var, frac, anchors, counts, *, n_band, n_lon):
@@ -154,16 +218,26 @@
     rows = -(-(levels + N_INFO) // 16) * 16
     half = rows // 2
     vmem = pl.BlockSpec(memory_space=pltpu.VMEM)
-    smem = pl.BlockSpec(memory_space=pltpu.SMEM)
+    hbm = pl.BlockSpec(memory_space=pltpu.HBM)
     params = pltpu.CompilerParams(vmem_limit_bytes=VMEM_LIMIT)
     struct = jax.ShapeDtypeStruct
 
     payload = pl.pallas_call(
         functools.partial(pack_kernel, cap=cap, lon_count=n_lon),
         out_shape=struct((devices, half, LANES), BF16),
-        in_specs=[smem] + [vmem] * 5,
-        out_specs=vmem,
-        compiler_params=params,
+        in_specs=[hbm] * 6,
+        out_specs=hbm,
+        scratch_shapes=[
+            pltpu.VMEM((devices, half, LANES), BF16),
+            pltpu.SMEM((1, devices), jnp.int32),
+            pltpu.VMEM((levels, slots), BF16),
+            pltpu.VMEM((1, slots), F32),
+            pltpu.VMEM((1, slots), F32),
+            pltpu.VMEM((2, slots), F32),
+            pltpu.VMEM((2, slots), jnp.int32),
+            pltpu.SemaphoreType.DMA((5 + 2 * JAC_CHUNKS,)),
+        ],
+        compiler_params=pltpu.CompilerParams(vmem_limit_bytes=VMEM_ALL),
         name="pack",
     )(counts, jacobian.T, departure[None, :], inv_var[None, :], frac, anchors)
 
@@ -200,7 +274,8 @@
         out_shape=struct((LAT_DEV, rows, LANES), F32),
         in_specs=[vmem] * 2,
         out_specs=vmem,
-        scratch_shapes=[pltpu.VMEM((LON_DEV, slots), BF16)] * 3,
+        scratch_shapes=[pltpu.VMEM((LON_DEV, slots), BF16)] * 2
+        + [pltpu.VMEM((LAT_DEV // SPAN * rows, slots), BF16)],
         compiler_params=params,
         cost_estimate=pl.CostEstimate(
             flops=2 * rows * slots * LAT_DEV * LON_DEV, bytes_accessed=4 * LAT_DEV * rows * LANES, transcendentals=0
@@ -208,14 +283,15 @@
         name="main",
     )(x, info)
 
-    block = rows // 3
     out = pl.pallas_call(
-        final_kernel,
-        grid=(3,),
+        functools.partial(final_kernel, levels=levels),
         out_shape=struct((levels * LAT_DEV, LON_DEV), F32),
-        in_specs=[pl.BlockSpec((LAT_DEV, block, LANES), lambda i: (0, i, 0))]
-        + [pl.BlockSpec((block, LANES), lambda i: (i, 0))] * 3,
-        out_specs=pl.BlockSpec((block * LAT_DEV, LON_DEV), lambda i: (i, 0)),
+        in_specs=[vmem] * 4,
+        out_specs=hbm,
+        scratch_shapes=[
+            pltpu.VMEM((rows * LAT_DEV, LON_DEV), F32),
+            pltpu.SemaphoreType.DMA((rows // STEP_LEVELS,)),
+        ],
         compiler_params=params,
         name="final",
     )(acc, east_in, north_in, corner_in)

time: 52.1 us -> 40.4 us (0.78)
  Pallas kernels: 16.5 us -> 9.38 us
  local copies, waits for them, and re-layouts: 4.54 us -> 0 us
    pallas_call x1, Pallas kernels: 10.9 us -> 3.31 us  [per_device(): pl.pallas_call(functools.partial(main_kernel, levels=levels), out_shape=s...]
    unnamed x12 -> x0, local copies, waits for them, and re-layouts: 4.54 us -> none
    pallas_call x1, Pallas kernels: 0.86 us -> 2.25 us  [per_device(): pl.pallas_call(functools.partial(pack_kernel, cap=cap, lon_count=n_lon),...]
    pallas_call x1, Pallas kernels: 3.71 us -> 2.79 us  [per_device(): pl.pallas_call(functools.partial(final_kernel, levels=levels), out_shape=...]
  transfers between devices with their start and end apart: 3 -> 3, of which waited for: 0 -> 0; matrix products, arithmetic and copies ran while one was open for 0% -> 0% of each run, Pallas kernels for 21% -> 8%
where the time goes in v2:
time: 40.4 us; the launch traced here: 40.1 us
  blocking collectives  24 us (59%)
  Pallas kernels  9.38 us (23%)
  starting transfers between devices  6.61 us (16%)
    all_to_all x1, blocking collectives, per_device(): lax.all_to_all(payload, ('band', 'lon'), split_axis=0, concat_axis=0, til...  24 us
    pallas_call x1, Pallas kernels, per_device(): pl.pallas_call(functools.partial(main_kernel, levels=levels), out_shape=s...  3.31 us
    pallas_call x1, Pallas kernels, per_device(): pl.pallas_call(functools.partial(final_kernel, levels=levels), out_shape=...  2.79 us
    ppermute x1, starting transfers between devices, per_device(): corner_in = lax.ppermute(east, ('band', 'lon'), corner_pairs)  2.57 us
    ppermute x1, starting transfers between devices, per_device(): lax.ppermute(north, 'band', [(i, i + 1) for i in range(n_band - 1)])  2.47 us
    pallas_call x1, Pallas kernels, per_device(): pl.pallas_call(functools.partial(pack_kernel, cap=cap, lon_count=n_lon),...  2.25 us
    ppermute x1, starting transfers between devices, per_device(): lax.ppermute(east, 'lon', [(j, (j + 1) % n_lon) for j in range(n_lon)])  1.57 us
    pallas_call x1, Pallas kernels, per_device(): pl.pallas_call(functools.partial(rim_kernel, cap=cap, levels=levels), out...  1.03 us
  transfers between devices with their start and end apart: 3, of which 0 were waited for; matrix products, arithmetic and copies ran while one was open for 0% of the time, Pallas kernels for 8%

profile of v2, /device:TPU:0, one launch (start us, length us, event | category | flops | bytes accessed | tf_op | source)
XLA Modules:
  0.0 40.1 jit_solution(16268526841543005754)
XLA Ops:
  0.0 2.2 %pack.1 = bf16[32,72,128]{2,1,0:T(8,128)(2,1)} custom-call(s32[1,32]{1,0:T(1,128)} %counts_hbm.1, bf16[137,2048]{1,0:T(8,128)(2,1)} %bitcast.4, f32[1,2048]{1,0:T(1,128)} %bitcast.5, f32[1,2048]{1,0:T(1,128)} %bitcast.6, f32[2,2048]{1,0:T(2,128)} %frac_hbm.1, s32[2,2048]{1,0:T(2,128)} %anchor_hbm.1), custom_call_target="tpu_custom_call" | custom-call | tf_op jit(solution)/shard_map/pack/pallas_call | solution.py:225
  2.3 24.0 %all_to_all.5.recv_ref = bf16[32,72,128]{2,1,0:T(8,128)(2,1)S(1)} all-to-all(bf16[32,72,128]{2,1,0:T(8,128)(2,1)} %pack.1), channel_id=1, replica_groups=mesh['band'=8,'lon'=4] {'band','lon'}, dimensions={0} | all-to-all | bytes 1179648 | tf_op jit(solution)/shard_map/all_to_all | solution.py:244
  26.3 1.0 %rim.1 = (bf16[144,2048]{1,0:T(8,128)(2,1)S(1)}, f32[8,2048]{1,0:T(8,128)S(1)}, f32[144,128]{1,0:T(8,128)S(1)}, f32[144,128]{1,0:T(8,128)S(1)}) custom-call(bf16[32,72,128]{2,1,0:T(8,128)(2,1)S(1)} %all_to_all.5.recv_ref), custom_call_target="tpu_custom_call" | custom-call | tf_op jit(solution)/shard_map/rim/pallas_call | solution.py:247
  27.3 2.6 %collective-permute-start.2 = (f32[144,128]{1,0:T(8,128)S(1)}, f32[144,128]{1,0:T(8,128)S(1)}, u32[]{:S(2)}, u32[]{:S(2)}) collective-permute-start(f32[144,128]{1,0:T(8,128)S(1)} %get-tuple-element.11), channel_id=1, source_target_pairs={{0,5},{1,6},{2,7},{3,4},{4,9},{5,10},{6,11},{7,8},{8,13},{9,14},{1... | collective-permute-start | bytes 221192 | tf_op jit(solution)/shard_map/ppermute | solution.py:268
  29.9 1.6 %collective-permute-start = (f32[144,128]{1,0:T(8,128)S(1)}, f32[144,128]{1,0:T(8,128)S(1)}, u32[]{:S(2)}, u32[]{:S(2)}) collective-permute-start(f32[144,128]{1,0:T(8,128)S(1)} %get-tuple-element.11), channel_id=1, source_target_pairs={{0,1},{1,2},{2,3},{3,0},{4,5},{5,6},{6,7},{7,4},{8,9},{9,10},{10,1... | collective-permute-start | bytes 221192 | tf_op jit(solution)/shard_map/ppermute | solution.py:269
  31.5 2.5 %collective-permute-start.1 = (f32[144,128]{1,0:T(8,128)S(1)}, f32[144,128]{1,0:T(8,128)S(1)}, u32[]{:S(2)}, u32[]{:S(2)}) collective-permute-start(f32[144,128]{1,0:T(8,128)S(1)} %get-tuple-element.12), channel_id=1, source_target_pairs={{0,4},{4,8},{8,12},{12,16},{16,20},{20,24},{24,28},{1,5},{5,9},{9,... | collective-permute-start | bytes 221192 | tf_op jit(solution)/shard_map/ppermute | solution.py:270
  34.0 3.3 %main.1.acc_ref = f32[32,144,128]{2,1,0:T(8,128)S(1)} custom-call(bf16[144,2048]{1,0:T(8,128)(2,1)S(1)} %get-tuple-element.9.x_ref, f32[8,2048]{1,0:T(8,128)S(1)} %get-tuple-element.10.info_ref), custom_call_target="tpu_custom_call" | custom-call | flops 2415919104 | bytes 2359296 | tf_op jit(solution)/shard_map/main/pallas_call | solution.py:272
  37.3 0.0 collective-permute-done.1.north_ref
  37.3 0.0 collective-permute-done.2.corner_ref
  37.3 0.0 collective-permute-done.east_ref
  37.3 2.8 %final.1 = f32[4384,128]{1,0:T(8,128)} custom-call(f32[32,144,128]{2,1,0:T(8,128)S(1)} %main.1.acc_ref, f32[144,128]{1,0:T(8,128)S(1)} %collective-permute-done.east_ref, f32[144,128]{1,0:T(8,128)S(1)} %collective-permute-done.1.north_ref, f32[144,128]{1,0:T(8,128)S(1)} %collective-permute-done.2.corner_ref), custom_call_target="tpu_custom_call" | custom-call | tf_op jit(solution)/shard_map/final/pallas_call | solution.py:286
Async XLA Ops:
  27.3 10.0 %collective-permute-start.2 = (f32[144,128]{1,0:T(8,128)S(1)}, f32[144,128]{1,0:T(8,128)S(1)}, u32[]{:S(2)}, u32[]{:S(2)}) collective-permute-start(f32[144,128]{1,0:T(8,128)S(1)} %get-tuple-element.11), channel_id=1, source_target_pairs={{0,5},{1,6},{2,7},{3,4},{4,9},{5,10},{6,11},{7,8},{8,13},{9,14},{1... | collective-permute-start | bytes 221192 | tf_op jit(solution)/shard_map/ppermute | solution.py:268
  29.9 7.4 %collective-permute-start = (f32[144,128]{1,0:T(8,128)S(1)}, f32[144,128]{1,0:T(8,128)S(1)}, u32[]{:S(2)}, u32[]{:S(2)}) collective-permute-start(f32[144,128]{1,0:T(8,128)S(1)} %get-tuple-element.11), channel_id=1, source_target_pairs={{0,1},{1,2},{2,3},{3,0},{4,5},{5,6},{6,7},{7,4},{8,9},{9,10},{10,1... | collective-permute-start | bytes 221192 | tf_op jit(solution)/shard_map/ppermute | solution.py:269
  31.5 5.8 %collective-permute-start.1 = (f32[144,128]{1,0:T(8,128)S(1)}, f32[144,128]{1,0:T(8,128)S(1)}, u32[]{:S(2)}, u32[]{:S(2)}) collective-permute-start(f32[144,128]{1,0:T(8,128)S(1)} %get-tuple-element.12), channel_id=1, source_target_pairs={{0,4},{4,8},{8,12},{12,16},{16,20},{20,24},{24,28},{1,5},{5,9},{9,... | collective-permute-start | bytes 221192 | tf_op jit(solution)/shard_map/ppermute | solution.py:270

commit v3 on v2

--- a/solution.py
+++ b/solution.py
@@ -14,10 +14,13 @@
 F32 = jnp.float32
 BF16 = jnp.bfloat16
 NT = (((1,), (1,)), ((), ()))
-VMEM_LIMIT = 48 * 1024 * 1024
+VMEM_LIMIT = 32 * 1024 * 1024
 VMEM_ALL = 64 * 1024 * 1024
 SPAN = 8
-STEP_LEVELS = 16
+GROUPS = LAT_DEV // SPAN
+LOWER = 4
+FOLD = 3
+PITCH = LANES // FOLD
 JAC_CHUNKS = 4
 
 
@@ -146,10 +149,28 @@
         ).astype(BF16)
     sums = lax.dot_general(x_ref[...], hot_ref[...], NT, preferred_element_type=F32)
     north_ref[...] = sums[:, :LON_DEV]
-    east_ref[...] = sums[:, LON_DEV:]
-
-
-def main_kernel(x_ref, info_ref, out_ref, near_ref, far_ref, left_ref, *, levels):
+    block = east_ref.shape[0]
+    east = sums[:block, LON_DEV:]
+    for g in range(1, FOLD):
+        east = east + pltpu.roll(sums[g * block : (g + 1) * block, LON_DEV:], g * PITCH, 1)
+    east_ref[...] = east
+
+
+def hot_rows(near_ref, far_ref, within, first, count):
+    zero = jnp.zeros(near_ref.shape, BF16)
+    hots = []
+    for v in range(first, first + count):
+        far_part = jnp.where(within == bf(v - 1), far_ref[...], zero) if v else zero
+        hots.append(jnp.where(within == bf(v), near_ref[...], far_part))
+    return jnp.concatenate(hots, axis=0)
+
+
+def split_latitude(lat):
+    group = jnp.floor(lat * (1.0 / SPAN))
+    return group.astype(BF16), (lat - group * SPAN).astype(BF16)
+
+
+def lower_kernel(x_ref, info_ref, acc_ref, near_ref, far_ref, left_ref, *, levels):
     rows, slots = x_ref.shape
     rest = levels % 8
     row = row_iota((LON_DEV, LANES)).astype(F32)
@@ -161,54 +182,78 @@
         near_ref[:, at] = jnp.where(here, w00, jnp.where(after, w01, 0.0)).astype(BF16)
         far_ref[:, at] = jnp.where(here, w10, jnp.where(after, w11, 0.0)).astype(BF16)
     lat = info_ref[rest + 4 : rest + 5, :]
-    group = jnp.floor(lat * (1.0 / SPAN))
-    within = (lat - group * SPAN).astype(BF16)
-    group = group.astype(BF16)
+    group, within = split_latitude(lat)
     lat = lat.astype(BF16)
-    groups = LAT_DEV // SPAN
     x = x_ref[...]
     zero_x = jnp.zeros_like(x)
-    for u in range(groups):
+    for u in range(GROUPS):
         left_ref[u * rows : (u + 1) * rows, :] = jnp.where(group == bf(u), x, zero_x)
     zero = jnp.zeros((LON_DEV, slots), BF16)
     far = far_ref[...]
-    hot = jnp.concatenate([jnp.where(lat == bf(SPAN * u - 1), far, zero) for u in range(1, groups)], axis=0)
+    hot = jnp.concatenate([jnp.where(lat == bf(SPAN * u - 1), far, zero) for u in range(1, GROUPS)], axis=0)
     seam = lax.dot_general(x, hot, NT, preferred_element_type=F32)
-    for first in range(0, SPAN, 2):
-        hots = []
-        for v in (first, first + 1):
-            far_part = jnp.where(within == bf(v - 1), far_ref[...], zero) if v else zero
-            hots.append(jnp.where(within == bf(v), near_ref[...], far_part))
-        sums = lax.dot_general(left_ref[...], jnp.concatenate(hots, axis=0), NT, preferred_element_type=F32)
-        for u in range(groups):
-            for v in (first, first + 1):
-                value = sums[u * rows : (u + 1) * rows, (v - first) * LON_DEV : (v - first + 1) * LON_DEV]
-                if v == 0 and u > 0:
+    for first in range(0, LOWER, 2):
+        hot = hot_rows(near_ref, far_ref, within, first, 2)
+        sums = lax.dot_general(left_ref[...], hot, NT, preferred_element_type=F32)
+        for u in range(GROUPS):
+            for i in range(2):
+                value = sums[u * rows : (u + 1) * rows, i * LON_DEV : (i + 1) * LON_DEV]
+                if first + i == 0 and u > 0:
                     value = value + seam[:, (u - 1) * LON_DEV : u * LON_DEV]
-                out_ref[u * SPAN + v] = value
-
-
-def final_kernel(acc_ref, east_ref, north_ref, corner_ref, out_hbm, out_ref, sems, *, levels):
+                acc_ref[u * LOWER + first + i] = value
+
+
+def edge_column(fold, r, first_lane):
+    parts = []
+    for g in range(FOLD):
+        shift = (LANES - g * PITCH - r) % LANES
+        parts.append(pltpu.roll(fold, shift, 1) if shift else fold)
+    return jnp.where(first_lane, jnp.concatenate(parts, axis=0), 0.0)
+
+
+def upper_kernel(
+    acc_ref, near_ref, far_ref, left_ref, info_ref, east_ref, out_hbm, south_ref, grid_ref, sems, *, levels
+):
     rows = acc_ref.shape[1]
-    lane = lane_iota((STEP_LEVELS, LANES))
-    first = lane == 0
+    rest = levels % 8
+    first_lane = lane_iota((rows, LANES)) == 0
     copies = []
-    for start in range(0, rows, STEP_LEVELS):
-        at = pl.ds(start, STEP_LEVELS)
-        east = east_ref[at, :]
-        for r in range(LAT_DEV):
-            value = acc_ref[r, at, :] + jnp.where(first, pltpu.roll(east, LANES - r, 1) if r else east, 0.0)
-            if r == 0:
-                value = value + north_ref[at, :]
-                value = value + jnp.where(first, pltpu.roll(corner_ref[at, :], LANES - LAT_DEV, 1), 0.0)
-            out_ref[pl.ds(start * LAT_DEV + r, STEP_LEVELS, LAT_DEV), :] = value
-        stop = min(start + STEP_LEVELS, levels)
-        span = pl.ds(start * LAT_DEV, (stop - start) * LAT_DEV)
-        copy = pltpu.make_async_copy(out_ref.at[span, :], out_hbm.at[span, :], sems.at[len(copies)])
+
+    def finish(r, value):
+        value = value + edge_column(east_ref[...], r, first_lane)
+        if r == 0:
+            south_ref[...] = value
+            return
+        grid_ref[r] = value
+        copy = pltpu.make_async_copy(grid_ref.at[r, 0:levels, :], out_hbm.at[:, r, :], sems.at[r])
         copy.start()
         copies.append(copy)
+
+    for u in range(GROUPS):
+        for v in range(LOWER):
+            finish(u * SPAN + v, acc_ref[u * LOWER + v])
+    _, within = split_latitude(info_ref[rest + 4 : rest + 5, :])
+    for first in range(LOWER, SPAN, 2):
+        hot = hot_rows(near_ref, far_ref, within, first, 2)
+        sums = lax.dot_general(left_ref[...], hot, NT, preferred_element_type=F32)
+        for u in range(GROUPS):
+            for i in range(2):
+                finish(
+                    u * SPAN + first + i,
+                    sums[u * rows : (u + 1) * rows, i * LON_DEV : (i + 1) * LON_DEV],
+                )
     for copy in copies:
         copy.wait()
+
+
+def last_kernel(south_ref, north_ref, corner_ref, grid_hbm, out_hbm, row_ref, sem):
+    del grid_hbm
+    first_lane = lane_iota(south_ref.shape) == 0
+    passed = north_ref[...] + edge_column(corner_ref[...], LAT_DEV, first_lane)
+    row_ref[...] = south_ref[...] + jnp.where(lax.axis_index("band") > 0, passed, 0.0)
+    copy = pltpu.make_async_copy(row_ref.at[0 : out_hbm.shape[0], :], out_hbm.at[:, 0, :], sem)
+    copy.start()
+    copy.wait()
 
 
 def per_device(jacobian, departure, inv_var, frac, anchors, counts, *, n_band, n_lon):
@@ -249,7 +294,7 @@
         out_shape=(
             struct((rows, slots), BF16),
             struct((tail_rows, slots), F32),
-            struct((rows, LANES), F32),
+            struct((rows // FOLD, LANES), F32),
             struct((rows, LANES), F32),
         ),
         in_specs=[vmem],
@@ -259,43 +304,49 @@
         name="rim",
     )(received)
 
-    def place(band, lon):
-        return band * n_lon + lon % n_lon
-
-    corner_pairs = [
-        (place(i, j), place(i + 1, j + 1)) for i in range(n_band - 1) for j in range(n_lon)
-    ]
-    corner_in = lax.ppermute(east, ("band", "lon"), corner_pairs)
-    east_in = lax.ppermute(east, "lon", [(j, (j + 1) % n_lon) for j in range(n_lon)])
-    north_in = lax.ppermute(north, "band", [(i, i + 1) for i in range(n_band - 1)])
-
-    acc = pl.pallas_call(
-        functools.partial(main_kernel, levels=levels),
-        out_shape=struct((LAT_DEV, rows, LANES), F32),
+    bands, lons = range(n_band), range(n_lon)
+    north_in = lax.ppermute(north, "band", [(i, (i + 1) % n_band) for i in bands])
+    corner_in = lax.ppermute(
+        east,
+        ("band", "lon"),
+        [(i * n_lon + j, (i + 1) % n_band * n_lon + (j + 1) % n_lon) for i in bands for j in lons],
+    )
+    east_in = lax.ppermute(east, "lon", [(j, (j + 1) % n_lon) for j in lons])
+
+    acc, near, far, left = pl.pallas_call(
+        functools.partial(lower_kernel, levels=levels),
+        out_shape=(
+            struct((GROUPS * LOWER, rows, LANES), F32),
+            struct((LON_DEV, slots), BF16),
+            struct((LON_DEV, slots), BF16),
+            struct((GROUPS * rows, slots), BF16),
+        ),
         in_specs=[vmem] * 2,
-        out_specs=vmem,
-        scratch_shapes=[pltpu.VMEM((LON_DEV, slots), BF16)] * 2
-        + [pltpu.VMEM((LAT_DEV // SPAN * rows, slots), BF16)],
+        out_specs=(vmem,) * 4,
         compiler_params=params,
-        cost_estimate=pl.CostEstimate(
-            flops=2 * rows * slots * LAT_DEV * LON_DEV, bytes_accessed=4 * LAT_DEV * rows * LANES, transcendentals=0
-        ),
-        name="main",
+        name="lower",
     )(x, info)
 
-    out = pl.pallas_call(
-        functools.partial(final_kernel, levels=levels),
-        out_shape=struct((levels * LAT_DEV, LON_DEV), F32),
-        in_specs=[vmem] * 4,
+    grid, south = pl.pallas_call(
+        functools.partial(upper_kernel, levels=levels),
+        out_shape=(struct((levels, LAT_DEV, LON_DEV), F32), struct((rows, LANES), F32)),
+        in_specs=[vmem] * 6,
+        out_specs=(hbm, vmem),
+        scratch_shapes=[pltpu.VMEM((LAT_DEV, rows, LANES), F32), pltpu.SemaphoreType.DMA((LAT_DEV,))],
+        compiler_params=params,
+        name="upper",
+    )(acc, near, far, left, info, east_in)
+
+    return pl.pallas_call(
+        last_kernel,
+        out_shape=struct((levels, LAT_DEV, LON_DEV), F32),
+        in_specs=[vmem, vmem, vmem, hbm],
         out_specs=hbm,
-        scratch_shapes=[
-            pltpu.VMEM((rows * LAT_DEV, LON_DEV), F32),
-            pltpu.SemaphoreType.DMA((rows // STEP_LEVELS,)),
-        ],
+        scratch_shapes=[pltpu.VMEM((rows, LANES), F32), pltpu.SemaphoreType.DMA],
+        input_output_aliases={3: 0},
         compiler_params=params,
-        name="final",
-    )(acc, east_in, north_in, corner_in)
-    return out.reshape(levels, LAT_DEV, LON_DEV)
+        name="last",
+    )(south, north_in, corner_in, grid)
 
 
 def solution(mesh):

time: 40.4 us -> 36.6 us (0.906)
  starting transfers between devices: 6.61 us -> 2.98 us
  Pallas kernels: 9.38 us -> 8.92 us
    ppermute x3, starting transfers between devices: 6.61 us -> 2.98 us  [the longest x1 1.6 us: per_device(): lax.ppermute(east, ('band', 'lon'), [(i * n_lon + j, (i + 1) % n_band * n...]
    pallas_call x2 -> x3, Pallas kernels: 6.1 us -> 5.57 us  [the longest x1 2.59 us: per_device(): pl.pallas_call(functools.partial(upper_kernel, levels=levels), out_shape=...]
  transfers between devices with their start and end apart: 3 -> 3, of which waited for: 0 -> 1; matrix products, arithmetic and copies ran while one was open for 0% -> 0% of each run, Pallas kernels for 8% -> 13%
where the time goes in v3:
time: 36.6 us; the launch traced here: 36.4 us
  blocking collectives  24 us (66%)
  Pallas kernels  8.92 us (24%)
  starting transfers between devices  2.98 us (8%)
  waiting for transfers between devices  0.39 us (1%)
    all_to_all x1, blocking collectives, per_device(): lax.all_to_all(payload, ('band', 'lon'), split_axis=0, concat_axis=0, til...  24 us
    pallas_call x1, Pallas kernels, per_device(): pl.pallas_call(functools.partial(upper_kernel, levels=levels), out_shape=...  2.59 us
    pallas_call x1, Pallas kernels, per_device(): pl.pallas_call(functools.partial(lower_kernel, levels=levels), out_shape=...  2.25 us
    pallas_call x1, Pallas kernels, per_device(): pl.pallas_call(functools.partial(pack_kernel, cap=cap, lon_count=n_lon),...  2.25 us
    ppermute x1, starting transfers between devices, per_device(): lax.ppermute(east, ('band', 'lon'), [(i * n_lon + j, (i + 1) % n_band * n...  1.6 us
    ppermute x1, starting transfers between devices, per_device(): lax.ppermute(north, 'band', [(i, (i + 1) % n_band) for i in bands])  1.38 us
    pallas_call x1, Pallas kernels, per_device(): pl.pallas_call(functools.partial(rim_kernel, cap=cap, levels=levels), out...  1.1 us
  transfers between devices with their start and end apart: 3, of which 1 were waited for; matrix products, arithmetic and copies ran while one was open for 0% of the time, Pallas kernels for 13%

profile of v3, /device:TPU:0, one launch (start us, length us, event | category | flops | bytes accessed | tf_op | source)
XLA Modules:
  0.0 36.4 jit_solution(14040707110729225140)
XLA Ops:
  0.0 2.2 %pack.1 = bf16[32,72,128]{2,1,0:T(8,128)(2,1)} custom-call(s32[1,32]{1,0:T(1,128)} %counts_hbm.1, bf16[137,2048]{1,0:T(8,128)(2,1)} %bitcast.3, f32[1,2048]{1,0:T(1,128)} %bitcast.4, f32[1,2048]{1,0:T(1,128)} %bitcast.5, f32[2,2048]{1,0:T(2,128)} %frac_hbm.1, s32[2,2048]{1,0:T(2,128)} %anchor_hbm.1), custom_call_target="tpu_custom_call" | custom-call | tf_op jit(solution)/shard_map/pack/pallas_call | solution.py:270
  2.3 24.0 %all_to_all.5.recv_ref = bf16[32,72,128]{2,1,0:T(8,128)(2,1)S(1)} all-to-all(bf16[32,72,128]{2,1,0:T(8,128)(2,1)} %pack.1), channel_id=1, replica_groups=mesh['band'=8,'lon'=4] {'band','lon'}, dimensions={0} | all-to-all | bytes 1179648 | tf_op jit(solution)/shard_map/all_to_all | solution.py:289
  26.3 1.1 %rim.1 = (bf16[144,2048]{1,0:T(8,128)(2,1)S(1)}, f32[8,2048]{1,0:T(8,128)S(1)}, f32[48,128]{1,0:T(8,128)S(1)}, f32[144,128]{1,0:T(8,128)S(1)}) custom-call(bf16[32,72,128]{2,1,0:T(8,128)(2,1)S(1)} %all_to_all.5.recv_ref), custom_call_target="tpu_custom_call" | custom-call | tf_op jit(solution)/shard_map/rim/pallas_call | solution.py:292
  27.4 1.4 %collective-permute-start.1 = (f32[144,128]{1,0:T(8,128)S(1)}, f32[144,128]{1,0:T(8,128)S(1)}, u32[]{:S(2)}, u32[]{:S(2)}) collective-permute-start(f32[144,128]{1,0:T(8,128)S(1)} %get-tuple-element.23), channel_id=1, source_target_pairs={{0,4},{4,8},{8,12},{12,16},{16,20},{20,24},{24,28},{28,0},{1,5},{5... | collective-permute-start | bytes 221192 | tf_op jit(solution)/shard_map/ppermute | solution.py:308
  28.8 0.0 collective-permute-start
  28.8 1.6 %collective-permute-start.2 = (f32[48,128]{1,0:T(8,128)S(1)}, f32[48,128]{1,0:T(8,128)S(1)}, u32[]{:S(2)}, u32[]{:S(2)}) collective-permute-start(f32[48,128]{1,0:T(8,128)S(1)} %get-tuple-element.21), channel_id=1, source_target_pairs={{0,5},{1,6},{2,7},{3,4},{4,9},{5,10},{6,11},{7,8},{8,13},{9,14},{1... | collective-permute-start | bytes 73736 | tf_op jit(solution)/shard_map/ppermute | solution.py:309
  30.4 2.3 %lower.1 = (f32[16,144,128]{2,1,0:T(8,128)S(1)}, bf16[128,2048]{1,0:T(8,128)(2,1)S(1)}, bf16[128,2048]{1,0:T(8,128)(2,1)S(1)}, bf16[576,2048]{1,0:T(8,128)(2,1)S(1)}) custom-call(bf16[144,2048]{1,0:T(8,128)(2,1)S(1)} %get-tuple-element.15.x_ref, f32[8,2048]{1,0:T(8,128)S(1)} %get-tuple-element.16.info_ref), custom_call_target="tpu_custom_call" | custom-call | tf_op jit(solution)/shard_map/lower/pallas_call | solution.py:316
  32.6 0.0 collective-permute-done.east_ref
  32.7 2.6 %upper.1 = (f32[137,32,128]{2,1,0:T(8,128)}, f32[144,128]{1,0:T(8,128)S(1)}) custom-call(f32[16,144,128]{2,1,0:T(8,128)S(1)} %get-tuple-element.17.acc_ref, bf16[128,2048]{1,0:T(8,128)(2,1)S(1)} %get-tuple-element.18.near_ref, bf16[128,2048]{1,0:T(8,128)(2,1)S(1)} %get-tuple-element.19.far_ref, bf16[576,2048]{1,0:T(8,128)(2,1)S(1)} %get-tuple-element.20.left_ref, ...), custom_call_target="tpu_custom_call" | custom-call | tf_op jit(solution)/shard_map/upper/pallas_call | solution.py:330
  35.3 0.4 %collective-permute-done.2.corner_ref = f32[48,128]{1,0:T(8,128)S(1)} collective-permute-done((f32[48,128]{1,0:T(8,128)S(1)}, f32[48,128]{1,0:T(8,128)S(1)}, u32[]{:S(2)}, u32[]{:S(2)}) %collective-permute-start.2) | collective-permute-done | bytes 24608 | tf_op jit(solution)/shard_map/ppermute | solution.py:309
  35.6 0.0 collective-permute-done.1.north_ref
  35.6 0.7 %last.1 = f32[137,32,128]{2,1,0:T(8,128)} custom-call(f32[144,128]{1,0:T(8,128)S(1)} %get-tuple-element.22.south_ref, f32[144,128]{1,0:T(8,128)S(1)} %collective-permute-done.1.north_ref, f32[48,128]{1,0:T(8,128)S(1)} %collective-permute-done.2.corner_ref, f32[137,32,128]{2,1,0:T(8,128)} %get-tuple-element.24.grid_hbm), custom_call_target="tpu_custom_call", output_to_operand_aliasing={{}: (3, {})} | custom-call | tf_op jit(solution)/shard_map/last/pallas_call | solution.py:340
Async XLA Ops:
  27.4 8.2 %collective-permute-start.1 = (f32[144,128]{1,0:T(8,128)S(1)}, f32[144,128]{1,0:T(8,128)S(1)}, u32[]{:S(2)}, u32[]{:S(2)}) collective-permute-start(f32[144,128]{1,0:T(8,128)S(1)} %get-tuple-element.23), channel_id=1, source_target_pairs={{0,4},{4,8},{8,12},{12,16},{16,20},{20,24},{24,28},{28,0},{1,5},{5... | collective-permute-start | bytes 221192 | tf_op jit(solution)/shard_map/ppermute | solution.py:308
  28.8 3.9 %collective-permute-start = (f32[48,128]{1,0:T(8,128)S(1)}, f32[48,128]{1,0:T(8,128)S(1)}, u32[]{:S(2)}, u32[]{:S(2)}) collective-permute-start(f32[48,128]{1,0:T(8,128)S(1)} %get-tuple-element.21), channel_id=1, source_target_pairs={{0,1},{1,2},{2,3},{3,0},{4,5},{5,6},{6,7},{7,4},{8,9},{9,10},{10,1... | collective-permute-start | bytes 73736 | tf_op jit(solution)/shard_map/ppermute | solution.py:314
  28.8 6.8 %collective-permute-start.2 = (f32[48,128]{1,0:T(8,128)S(1)}, f32[48,128]{1,0:T(8,128)S(1)}, u32[]{:S(2)}, u32[]{:S(2)}) collective-permute-start(f32[48,128]{1,0:T(8,128)S(1)} %get-tuple-element.21), channel_id=1, source_target_pairs={{0,5},{1,6},{2,7},{3,4},{4,9},{5,10},{6,11},{7,8},{8,13},{9,14},{1... | collective-permute-start | bytes 73736 | tf_op jit(solution)/shard_map/ppermute | solution.py:309

commit v4 on v3

--- a/solution.py
+++ b/solution.py
@@ -18,10 +18,11 @@
 VMEM_ALL = 64 * 1024 * 1024
 SPAN = 8
 GROUPS = LAT_DEV // SPAN
-LOWER = 4
+LOWER = 6
+EDGE_ROWS = -(-(LAT_DEV + 1) // 16) * 16
 FOLD = 3
 PITCH = LANES // FOLD
-JAC_CHUNKS = 4
+JAC_CHUNKS = 2
 
 
 def bf(value):
@@ -122,7 +123,7 @@
         copy.wait()
 
 
-def rim_kernel(recv_ref, x_ref, info_ref, east_ref, north_ref, hot_ref, *, cap, levels):
+def rim_kernel(recv_ref, x_ref, info_ref, east_ref, north_ref, corner_ref, hot_ref, *, cap, levels):
     devices, half, _ = recv_ref.shape
     body = (levels // 8) * 8
     rest = levels - body
@@ -144,16 +145,20 @@
         edge = lon == LON_DEV - 1.0
         w01 = jnp.where(edge, w01, 0.0)
         w11 = jnp.where(edge, w11, 0.0)
-        hot_ref[LON_DEV:, at] = jnp.where(
-            row == lat, w01, jnp.where(row == lat + 1.0, w11, 0.0)
+        few = row[:EDGE_ROWS]
+        hot_ref[LON_DEV : LON_DEV + EDGE_ROWS, at] = jnp.where(
+            few == lat, w01, jnp.where(few == lat + 1.0, w11, 0.0)
         ).astype(BF16)
+    hot_ref[LON_DEV + EDGE_ROWS :, :] = jnp.zeros((LANES - EDGE_ROWS, x_ref.shape[1]), BF16)
     sums = lax.dot_general(x_ref[...], hot_ref[...], NT, preferred_element_type=F32)
-    north_ref[...] = sums[:, :LON_DEV]
+    north_ref[...] = sums[:, :LON_DEV].astype(BF16)
     block = east_ref.shape[0]
     east = sums[:block, LON_DEV:]
     for g in range(1, FOLD):
         east = east + pltpu.roll(sums[g * block : (g + 1) * block, LON_DEV:], g * PITCH, 1)
     east_ref[...] = east
+    corner_ref[:block] = east
+    corner_ref[block:] = east
 
 
 def hot_rows(near_ref, far_ref, within, first, count):
@@ -249,7 +254,7 @@
 def last_kernel(south_ref, north_ref, corner_ref, grid_hbm, out_hbm, row_ref, sem):
     del grid_hbm
     first_lane = lane_iota(south_ref.shape) == 0
-    passed = north_ref[...] + edge_column(corner_ref[...], LAT_DEV, first_lane)
+    passed = north_ref[...].astype(F32) + edge_column(corner_ref[: corner_ref.shape[0] // 2], LAT_DEV, first_lane)
     row_ref[...] = south_ref[...] + jnp.where(lax.axis_index("band") > 0, passed, 0.0)
     copy = pltpu.make_async_copy(row_ref.at[0 : out_hbm.shape[0], :], out_hbm.at[:, 0, :], sem)
     copy.start()
@@ -289,16 +294,17 @@
     received = lax.all_to_all(payload, ("band", "lon"), split_axis=0, concat_axis=0, tiled=True)
 
     tail_rows = rows - levels // 8 * 8
-    x, info, east, north = pl.pallas_call(
+    x, info, east, north, corner = pl.pallas_call(
         functools.partial(rim_kernel, cap=cap, levels=levels),
         out_shape=(
             struct((rows, slots), BF16),
             struct((tail_rows, slots), F32),
             struct((rows // FOLD, LANES), F32),
-            struct((rows, LANES), F32),
+            struct((rows, LANES), BF16),
+            struct((rows // FOLD * 2, LANES), F32),
         ),
         in_specs=[vmem],
-        out_specs=(vmem,) * 4,
+        out_specs=(vmem,) * 5,
         scratch_shapes=[pltpu.VMEM((2 * LANES, slots), BF16)],
         compiler_params=params,
         name="rim",
@@ -307,7 +313,7 @@
     bands, lons = range(n_band), range(n_lon)
     north_in = lax.ppermute(north, "band", [(i, (i + 1) % n_band) for i in bands])
     corner_in = lax.ppermute(
-        east,
+        corner,
         ("band", "lon"),
         [(i * n_lon + j, (i + 1) % n_band * n_lon + (j + 1) % n_lon) for i in bands for j in lons],
     )

time: 36.6 us -> 35.9 us (0.981)
  starting transfers between devices: 2.98 us -> 2.53 us
  Pallas kernels: 8.92 us -> 8.55 us
    ppermute x1, starting transfers between devices: 1.6 us -> 0.71 us  [per_device(): lax.ppermute(corner, ('band', 'lon'), [(i * n_lon + j, (i + 1) % n_band *...]
    pallas_call x1, Pallas kernels: 2.59 us -> 1.83 us  [per_device(): pl.pallas_call(functools.partial(upper_kernel, levels=levels), out_shape=...]
    pallas_call x1, Pallas kernels: 2.25 us -> 2.86 us  [per_device(): pl.pallas_call(functools.partial(lower_kernel, levels=levels), out_shape=...]
  transfers between devices with their start and end apart: 3 -> 3, of which waited for: 1 -> 2; matrix products, arithmetic and copies ran while one was open for 0% -> 0% of each run, Pallas kernels for 13% -> 13%
where the time goes in v4:
time: 35.9 us; the launch traced here: 35.5 us
  blocking collectives  24 us (67%)
  Pallas kernels  8.55 us (24%)
  starting transfers between devices  2.53 us (7%)
  waiting for transfers between devices  0.38 us (1%)
    all_to_all x1, blocking collectives, per_device(): lax.all_to_all(payload, ('band', 'lon'), split_axis=0, concat_axis=0, til...  24 us
    pallas_call x1, Pallas kernels, per_device(): pl.pallas_call(functools.partial(lower_kernel, levels=levels), out_shape=...  2.86 us
    pallas_call x1, Pallas kernels, per_device(): pl.pallas_call(functools.partial(pack_kernel, cap=cap, lon_count=n_lon),...  2.16 us
    pallas_call x1, Pallas kernels, per_device(): pl.pallas_call(functools.partial(upper_kernel, levels=levels), out_shape=...  1.83 us
    ppermute x1, starting transfers between devices, per_device(): lax.ppermute(north, 'band', [(i, (i + 1) % n_band) for i in bands])  1.48 us
    pallas_call x1, Pallas kernels, per_device(): pl.pallas_call(functools.partial(rim_kernel, cap=cap, levels=levels), out...  0.96 us
    pallas_call x1, Pallas kernels, per_device(): pl.pallas_call(last_kernel, out_shape=struct((levels, LAT_DEV, LON_DEV),...  0.73 us
  transfers between devices with their start and end apart: 3, of which 2 were waited for; matrix products, arithmetic and copies ran while one was open for 0% of the time, Pallas kernels for 13%

profile of v4, /device:TPU:0, one launch (start us, length us, event | category | flops | bytes accessed | tf_op | source)
XLA Modules:
  0.0 35.5 jit_solution(928673788473812630)
XLA Ops:
  0.0 2.2 %pack.1 = bf16[32,72,128]{2,1,0:T(8,128)(2,1)} custom-call(s32[1,32]{1,0:T(1,128)} %counts_hbm.1, bf16[137,2048]{1,0:T(8,128)(2,1)} %bitcast.3, f32[1,2048]{1,0:T(1,128)} %bitcast.4, f32[1,2048]{1,0:T(1,128)} %bitcast.5, f32[2,2048]{1,0:T(2,128)} %frac_hbm.1, s32[2,2048]{1,0:T(2,128)} %anchor_hbm.1), custom_call_target="tpu_custom_call" | custom-call | tf_op jit(solution)/shard_map/pack/pallas_call | solution.py:275
  2.2 24.0 %all_to_all.5.recv_ref = bf16[32,72,128]{2,1,0:T(8,128)(2,1)S(1)} all-to-all(bf16[32,72,128]{2,1,0:T(8,128)(2,1)} %pack.1), channel_id=1, replica_groups=mesh['band'=8,'lon'=4] {'band','lon'}, dimensions={0} | all-to-all | bytes 1179648 | tf_op jit(solution)/shard_map/all_to_all | solution.py:294
  26.2 1.0 %rim.1 = (bf16[144,2048]{1,0:T(8,128)(2,1)S(1)}, f32[8,2048]{1,0:T(8,128)S(1)}, f32[48,128]{1,0:T(8,128)S(1)}, bf16[144,128]{1,0:T(8,128)(2,1)S(1)}, f32[96,128]{1,0:T(8,128)S(1)}) custom-call(bf16[32,72,128]{2,1,0:T(8,128)(2,1)S(1)} %all_to_all.5.recv_ref), custom_call_target="tpu_custom_call" | custom-call | tf_op jit(solution)/shard_map/rim/pallas_call | solution.py:297
  27.2 0.7 %collective-permute-start.2 = (f32[96,128]{1,0:T(8,128)S(1)}, f32[96,128]{1,0:T(8,128)S(1)}, u32[]{:S(2)}, u32[]{:S(2)}) collective-permute-start(f32[96,128]{1,0:T(8,128)S(1)} %get-tuple-element.25), channel_id=1, source_target_pairs={{0,5},{1,6},{2,7},{3,4},{4,9},{5,10},{6,11},{7,8},{8,13},{9,14},{1... | collective-permute-start | bytes 147464 | tf_op jit(solution)/shard_map/ppermute | solution.py:315
  27.9 1.5 %collective-permute-start.1 = (bf16[144,128]{1,0:T(8,128)(2,1)S(1)}, bf16[144,128]{1,0:T(8,128)(2,1)S(1)}, u32[]{:S(2)}, u32[]{:S(2)}) collective-permute-start(bf16[144,128]{1,0:T(8,128)(2,1)S(1)} %get-tuple-element.24), channel_id=1, source_target_pairs={{0,4},{4,8},{8,12},{12,16},{16,20},{20,24},{24,28},{28,0},{1,5},{5... | collective-permute-start | bytes 110600 | tf_op jit(solution)/shard_map/ppermute | solution.py:314
  29.4 0.3 collective-permute-start
  29.7 2.9 %lower.1 = (f32[24,144,128]{2,1,0:T(8,128)S(1)}, bf16[128,2048]{1,0:T(8,128)(2,1)S(1)}, bf16[128,2048]{1,0:T(8,128)(2,1)S(1)}, bf16[576,2048]{1,0:T(8,128)(2,1)S(1)}) custom-call(bf16[144,2048]{1,0:T(8,128)(2,1)S(1)} %get-tuple-element.16.x_ref, f32[8,2048]{1,0:T(8,128)S(1)} %get-tuple-element.17.info_ref), custom_call_target="tpu_custom_call" | custom-call | tf_op jit(solution)/shard_map/lower/pallas_call | solution.py:322
  32.6 0.0 collective-permute-done.east_ref
  32.6 1.8 %upper.1 = (f32[137,32,128]{2,1,0:T(8,128)}, f32[144,128]{1,0:T(8,128)S(1)}) custom-call(f32[24,144,128]{2,1,0:T(8,128)S(1)} %get-tuple-element.18.acc_ref, bf16[128,2048]{1,0:T(8,128)(2,1)S(1)} %get-tuple-element.19.near_ref, bf16[128,2048]{1,0:T(8,128)(2,1)S(1)} %get-tuple-element.20.far_ref, bf16[576,2048]{1,0:T(8,128)(2,1)S(1)} %get-tuple-element.21.left_ref, ...), custom_call_target="tpu_custom_call" | custom-call | tf_op jit(solution)/shard_map/upper/pallas_call | solution.py:336
  34.5 0.3 collective-permute-done.1.north_ref
  34.8 0.1 collective-permute-done.2.corner_ref
  34.8 0.7 %last.1 = f32[137,32,128]{2,1,0:T(8,128)} custom-call(f32[144,128]{1,0:T(8,128)S(1)} %get-tuple-element.23.south_ref, bf16[144,128]{1,0:T(8,128)(2,1)S(1)} %collective-permute-done.1.north_ref, f32[96,128]{1,0:T(8,128)S(1)} %collective-permute-done.2.corner_ref, f32[137,32,128]{2,1,0:T(8,128)} %get-tuple-element.26.grid_hbm), custom_call_target="tpu_custom_call", output_to_operand_aliasing={{}: (3, {})} | custom-call | tf_op jit(solution)/shard_map/last/pallas_call | solution.py:346
Async XLA Ops:
  27.2 7.6 %collective-permute-start.2 = (f32[96,128]{1,0:T(8,128)S(1)}, f32[96,128]{1,0:T(8,128)S(1)}, u32[]{:S(2)}, u32[]{:S(2)}) collective-permute-start(f32[96,128]{1,0:T(8,128)S(1)} %get-tuple-element.25), channel_id=1, source_target_pairs={{0,5},{1,6},{2,7},{3,4},{4,9},{5,10},{6,11},{7,8},{8,13},{9,14},{1... | collective-permute-start | bytes 147464 | tf_op jit(solution)/shard_map/ppermute | solution.py:315
  27.9 6.9 %collective-permute-start.1 = (bf16[144,128]{1,0:T(8,128)(2,1)S(1)}, bf16[144,128]{1,0:T(8,128)(2,1)S(1)}, u32[]{:S(2)}, u32[]{:S(2)}) collective-permute-start(bf16[144,128]{1,0:T(8,128)(2,1)S(1)} %get-tuple-element.24), channel_id=1, source_target_pairs={{0,4},{4,8},{8,12},{12,16},{16,20},{20,24},{24,28},{28,0},{1,5},{5... | collective-permute-start | bytes 110600 | tf_op jit(solution)/shard_map/ppermute | solution.py:314
  29.4 3.3 %collective-permute-start = (f32[48,128]{1,0:T(8,128)S(1)}, f32[48,128]{1,0:T(8,128)S(1)}, u32[]{:S(2)}, u32[]{:S(2)}) collective-permute-start(f32[48,128]{1,0:T(8,128)S(1)} %get-tuple-element.22), channel_id=1, source_target_pairs={{0,1},{1,2},{2,3},{3,0},{4,5},{5,6},{6,7},{7,4},{8,9},{9,10},{10,1... | collective-permute-start | bytes 73736 | tf_op jit(solution)/shard_map/ppermute | solution.py:320

commit v5 on v4

--- a/solution.py
+++ b/solution.py
@@ -16,9 +16,9 @@
 NT = (((1,), (1,)), ((), ()))
 VMEM_LIMIT = 32 * 1024 * 1024
 VMEM_ALL = 64 * 1024 * 1024
-SPAN = 8
+SPAN = 16
 GROUPS = LAT_DEV // SPAN
-LOWER = 6
+LOWER = 12
 EDGE_ROWS = -(-(LAT_DEV + 1) // 16) * 16
 FOLD = 3
 PITCH = LANES // FOLD
@@ -158,7 +158,7 @@
         east = east + pltpu.roll(sums[g * block : (g + 1) * block, LON_DEV:], g * PITCH, 1)
     east_ref[...] = east
     corner_ref[:block] = east
-    corner_ref[block:] = east
+    corner_ref[block:] = east[:32]
 
 
 def hot_rows(near_ref, far_ref, within, first, count):
@@ -254,7 +254,7 @@
 def last_kernel(south_ref, north_ref, corner_ref, grid_hbm, out_hbm, row_ref, sem):
     del grid_hbm
     first_lane = lane_iota(south_ref.shape) == 0
-    passed = north_ref[...].astype(F32) + edge_column(corner_ref[: corner_ref.shape[0] // 2], LAT_DEV, first_lane)
+    passed = north_ref[...].astype(F32) + edge_column(corner_ref[: south_ref.shape[0] // FOLD], LAT_DEV, first_lane)
     row_ref[...] = south_ref[...] + jnp.where(lax.axis_index("band") > 0, passed, 0.0)
     copy = pltpu.make_async_copy(row_ref.at[0 : out_hbm.shape[0], :], out_hbm.at[:, 0, :], sem)
     copy.start()
@@ -301,7 +301,7 @@
             struct((tail_rows, slots), F32),
             struct((rows // FOLD, LANES), F32),
             struct((rows, LANES), BF16),
-            struct((rows // FOLD * 2, LANES), F32),
+            struct((rows // FOLD + 32, LANES), F32),
         ),
         in_specs=[vmem],
         out_specs=(vmem,) * 5,

time: 35.9 us -> 35.7 us (level)
  no operation moved by 1% of the time
where the time goes in v5:
time: 35.7 us; the launch traced here: 35.5 us
  blocking collectives  24 us (67%)
  Pallas kernels  8.33 us (23%)
  starting transfers between devices  2.53 us (7%)
  waiting for transfers between devices  0.51 us (1%)
    all_to_all x1, blocking collectives, per_device(): lax.all_to_all(payload, ('band', 'lon'), split_axis=0, concat_axis=0, til...  24 us
    pallas_call x1, Pallas kernels, per_device(): pl.pallas_call(functools.partial(lower_kernel, levels=levels), out_shape=...  2.59 us
    pallas_call x1, Pallas kernels, per_device(): pl.pallas_call(functools.partial(pack_kernel, cap=cap, lon_count=n_lon),...  2.16 us
    pallas_call x1, Pallas kernels, per_device(): pl.pallas_call(functools.partial(upper_kernel, levels=levels), out_shape=...  1.89 us
    ppermute x1, starting transfers between devices, per_device(): lax.ppermute(north, 'band', [(i, (i + 1) % n_band) for i in bands])  1.48 us
    pallas_call x1, Pallas kernels, per_device(): pl.pallas_call(functools.partial(rim_kernel, cap=cap, levels=levels), out...  0.96 us
    pallas_call x1, Pallas kernels, per_device(): pl.pallas_call(last_kernel, out_shape=struct((levels, LAT_DEV, LON_DEV),...  0.73 us
  transfers between devices with their start and end apart: 3, of which 2 were waited for; matrix products, arithmetic and copies ran while one was open for 0% of the time, Pallas kernels for 13%

profile of v5, /device:TPU:0, one launch (start us, length us, event | category | flops | bytes accessed | tf_op | source)
XLA Modules:
  0.0 35.5 jit_solution(15823146973173156707)
XLA Ops:
  0.0 2.2 %pack.1 = bf16[32,72,128]{2,1,0:T(8,128)(2,1)} custom-call(s32[1,32]{1,0:T(1,128)} %counts_hbm.1, bf16[137,2048]{1,0:T(8,128)(2,1)} %bitcast.3, f32[1,2048]{1,0:T(1,128)} %bitcast.4, f32[1,2048]{1,0:T(1,128)} %bitcast.5, f32[2,2048]{1,0:T(2,128)} %frac_hbm.1, s32[2,2048]{1,0:T(2,128)} %anchor_hbm.1), custom_call_target="tpu_custom_call" | custom-call | tf_op jit(solution)/shard_map/pack/pallas_call | solution.py:275
  2.2 24.0 %all_to_all.5.recv_ref = bf16[32,72,128]{2,1,0:T(8,128)(2,1)S(1)} all-to-all(bf16[32,72,128]{2,1,0:T(8,128)(2,1)} %pack.1), channel_id=1, replica_groups=mesh['band'=8,'lon'=4] {'band','lon'}, dimensions={0} | all-to-all | bytes 1179648 | tf_op jit(solution)/shard_map/all_to_all | solution.py:294
  26.2 1.0 %rim.1 = (bf16[144,2048]{1,0:T(8,128)(2,1)S(1)}, f32[8,2048]{1,0:T(8,128)S(1)}, f32[48,128]{1,0:T(8,128)S(1)}, bf16[144,128]{1,0:T(8,128)(2,1)S(1)}, f32[80,128]{1,0:T(8,128)S(1)}) custom-call(bf16[32,72,128]{2,1,0:T(8,128)(2,1)S(1)} %all_to_all.5.recv_ref), custom_call_target="tpu_custom_call" | custom-call | tf_op jit(solution)/shard_map/rim/pallas_call | solution.py:297
  27.2 0.7 %collective-permute-start.2 = (f32[80,128]{1,0:T(8,128)S(1)}, f32[80,128]{1,0:T(8,128)S(1)}, u32[]{:S(2)}, u32[]{:S(2)}) collective-permute-start(f32[80,128]{1,0:T(8,128)S(1)} %get-tuple-element.25), channel_id=1, source_target_pairs={{0,5},{1,6},{2,7},{3,4},{4,9},{5,10},{6,11},{7,8},{8,13},{9,14},{1... | collective-permute-start | bytes 122888 | tf_op jit(solution)/shard_map/ppermute | solution.py:315
  27.9 1.5 %collective-permute-start.1 = (bf16[144,128]{1,0:T(8,128)(2,1)S(1)}, bf16[144,128]{1,0:T(8,128)(2,1)S(1)}, u32[]{:S(2)}, u32[]{:S(2)}) collective-permute-start(bf16[144,128]{1,0:T(8,128)(2,1)S(1)} %get-tuple-element.24), channel_id=1, source_target_pairs={{0,4},{4,8},{8,12},{12,16},{16,20},{20,24},{24,28},{28,0},{1,5},{5... | collective-permute-start | bytes 110600 | tf_op jit(solution)/shard_map/ppermute | solution.py:314
  29.4 0.3 collective-permute-start
  29.7 2.6 %lower.1 = (f32[24,144,128]{2,1,0:T(8,128)S(1)}, bf16[128,2048]{1,0:T(8,128)(2,1)S(1)}, bf16[128,2048]{1,0:T(8,128)(2,1)S(1)}, bf16[288,2048]{1,0:T(8,128)(2,1)S(1)}) custom-call(bf16[144,2048]{1,0:T(8,128)(2,1)S(1)} %get-tuple-element.16.x_ref, f32[8,2048]{1,0:T(8,128)S(1)} %get-tuple-element.17.info_ref), custom_call_target="tpu_custom_call" | custom-call | tf_op jit(solution)/shard_map/lower/pallas_call | solution.py:322
  32.3 0.3 collective-permute-done.east_ref
  32.6 1.9 %upper.1 = (f32[137,32,128]{2,1,0:T(8,128)}, f32[144,128]{1,0:T(8,128)S(1)}) custom-call(f32[24,144,128]{2,1,0:T(8,128)S(1)} %get-tuple-element.18.acc_ref, bf16[128,2048]{1,0:T(8,128)(2,1)S(1)} %get-tuple-element.19.near_ref, bf16[128,2048]{1,0:T(8,128)(2,1)S(1)} %get-tuple-element.20.far_ref, bf16[288,2048]{1,0:T(8,128)(2,1)S(1)} %get-tuple-element.21.left_ref, ...), custom_call_target="tpu_custom_call" | custom-call | tf_op jit(solution)/shard_map/upper/pallas_call | solution.py:336
  34.5 0.2 collective-permute-done.1.north_ref
  34.7 0.0 collective-permute-done.2.corner_ref
  34.7 0.7 %last.1 = f32[137,32,128]{2,1,0:T(8,128)} custom-call(f32[144,128]{1,0:T(8,128)S(1)} %get-tuple-element.23.south_ref, bf16[144,128]{1,0:T(8,128)(2,1)S(1)} %collective-permute-done.1.north_ref, f32[80,128]{1,0:T(8,128)S(1)} %collective-permute-done.2.corner_ref, f32[137,32,128]{2,1,0:T(8,128)} %get-tuple-element.26.grid_hbm), custom_call_target="tpu_custom_call", output_to_operand_aliasing={{}: (3, {})} | custom-call | tf_op jit(solution)/shard_map/last/pallas_call | solution.py:346
Async XLA Ops:
  27.2 7.5 %collective-permute-start.2 = (f32[80,128]{1,0:T(8,128)S(1)}, f32[80,128]{1,0:T(8,128)S(1)}, u32[]{:S(2)}, u32[]{:S(2)}) collective-permute-start(f32[80,128]{1,0:T(8,128)S(1)} %get-tuple-element.25), channel_id=1, source_target_pairs={{0,5},{1,6},{2,7},{3,4},{4,9},{5,10},{6,11},{7,8},{8,13},{9,14},{1... | collective-permute-start | bytes 122888 | tf_op jit(solution)/shard_map/ppermute | solution.py:315
  27.9 6.8 %collective-permute-start.1 = (bf16[144,128]{1,0:T(8,128)(2,1)S(1)}, bf16[144,128]{1,0:T(8,128)(2,1)S(1)}, u32[]{:S(2)}, u32[]{:S(2)}) collective-permute-start(bf16[144,128]{1,0:T(8,128)(2,1)S(1)} %get-tuple-element.24), channel_id=1, source_target_pairs={{0,4},{4,8},{8,12},{12,16},{16,20},{20,24},{24,28},{28,0},{1,5},{5... | collective-permute-start | bytes 110600 | tf_op jit(solution)/shard_map/ppermute | solution.py:314
  29.4 3.3 %collective-permute-start = (f32[48,128]{1,0:T(8,128)S(1)}, f32[48,128]{1,0:T(8,128)S(1)}, u32[]{:S(2)}, u32[]{:S(2)}) collective-permute-start(f32[48,128]{1,0:T(8,128)S(1)} %get-tuple-element.22), channel_id=1, source_target_pairs={{0,1},{1,2},{2,3},{3,0},{4,5},{5,6},{6,7},{7,4},{8,9},{9,10},{10,1... | collective-permute-start | bytes 73736 | tf_op jit(solution)/shard_map/ppermute | solution.py:320

commit v6 on v5

--- a/solution.py
+++ b/solution.py
@@ -74,7 +74,7 @@
         )
         for i in range(JAC_CHUNKS)
     ]
-    for copy in small + large:
+    for copy in large + small:
         copy.start()
     for copy in small:
         copy.wait()
@@ -315,7 +315,11 @@
     corner_in = lax.ppermute(
         corner,
         ("band", "lon"),
-        [(i * n_lon + j, (i + 1) % n_band * n_lon + (j + 1) % n_lon) for i in bands for j in lons],
+        [
+            (i * n_lon + j, (i + 1) % n_band * n_lon + (j + (i + 1 < n_band)) % n_lon)
+            for i in bands
+            for j in lons
+        ],
     )
     east_in = lax.ppermute(east, "lon", [(j, (j + 1) % n_lon) for j in lons])
 

time: 35.7 us -> 35.7 us (level)
  transfers between devices with their start and end apart: 3 -> 3, of which waited for: 2 -> 1; matrix products, arithmetic and copies ran while one was open for 0% -> 0% of each run, Pallas kernels for 13% -> 13%
where the time goes in v6:
time: 35.7 us; the launch traced here: 35.2 us
  blocking collectives  24 us (67%)
  Pallas kernels  8.29 us (23%)
  starting transfers between devices  2.53 us (7%)
    all_to_all x1, blocking collectives, per_device(): lax.all_to_all(payload, ('band', 'lon'), split_axis=0, concat_axis=0, til...  24 us
    pallas_call x1, Pallas kernels, per_device(): pl.pallas_call(functools.partial(lower_kernel, levels=levels), out_shape=...  2.59 us
    pallas_call x1, Pallas kernels, per_device(): pl.pallas_call(functools.partial(pack_kernel, cap=cap, lon_count=n_lon),...  2.12 us
    pallas_call x1, Pallas kernels, per_device(): pl.pallas_call(functools.partial(upper_kernel, levels=levels), out_shape=...  1.88 us
    ppermute x1, starting transfers between devices, per_device(): lax.ppermute(north, 'band', [(i, (i + 1) % n_band) for i in bands])  1.48 us
    pallas_call x1, Pallas kernels, per_device(): pl.pallas_call(functools.partial(rim_kernel, cap=cap, levels=levels), out...  0.96 us
    pallas_call x1, Pallas kernels, per_device(): pl.pallas_call(last_kernel, out_shape=struct((levels, LAT_DEV, LON_DEV),...  0.73 us
    ppermute x1, starting transfers between devices, per_device(): lax.ppermute(corner, ('band', 'lon'), [(i * n_lon + j, (i + 1) % n_band *...  0.71 us
  transfers between devices with their start and end apart: 3, of which 1 were waited for; matrix products, arithmetic and copies ran while one was open for 0% of the time, Pallas kernels for 13%

profile of v6, /device:TPU:0, one launch (start us, length us, event | category | flops | bytes accessed | tf_op | source)
XLA Modules:
  0.0 35.2 jit_solution(694447115748159152)
XLA Ops:
  0.0 2.1 %pack.1 = bf16[32,72,128]{2,1,0:T(8,128)(2,1)} custom-call(s32[1,32]{1,0:T(1,128)} %counts_hbm.1, bf16[137,2048]{1,0:T(8,128)(2,1)} %bitcast.3, f32[1,2048]{1,0:T(1,128)} %bitcast.4, f32[1,2048]{1,0:T(1,128)} %bitcast.5, f32[2,2048]{1,0:T(2,128)} %frac_hbm.1, s32[2,2048]{1,0:T(2,128)} %anchor_hbm.1), custom_call_target="tpu_custom_call" | custom-call | tf_op jit(solution)/shard_map/pack/pallas_call | solution.py:275
  2.1 24.0 %all_to_all.5.recv_ref = bf16[32,72,128]{2,1,0:T(8,128)(2,1)S(1)} all-to-all(bf16[32,72,128]{2,1,0:T(8,128)(2,1)} %pack.1), channel_id=1, replica_groups=mesh['band'=8,'lon'=4] {'band','lon'}, dimensions={0} | all-to-all | bytes 1179648 | tf_op jit(solution)/shard_map/all_to_all | solution.py:294
  26.2 1.0 %rim.1 = (bf16[144,2048]{1,0:T(8,128)(2,1)S(1)}, f32[8,2048]{1,0:T(8,128)S(1)}, f32[48,128]{1,0:T(8,128)S(1)}, bf16[144,128]{1,0:T(8,128)(2,1)S(1)}, f32[80,128]{1,0:T(8,128)S(1)}) custom-call(bf16[32,72,128]{2,1,0:T(8,128)(2,1)S(1)} %all_to_all.5.recv_ref), custom_call_target="tpu_custom_call" | custom-call | tf_op jit(solution)/shard_map/rim/pallas_call | solution.py:297
  27.1 0.7 %collective-permute-start.2 = (f32[80,128]{1,0:T(8,128)S(1)}, f32[80,128]{1,0:T(8,128)S(1)}, u32[]{:S(2)}, u32[]{:S(2)}) collective-permute-start(f32[80,128]{1,0:T(8,128)S(1)} %get-tuple-element.25), channel_id=1, source_target_pairs={{0,5},{1,6},{2,7},{3,4},{4,9},{5,10},{6,11},{7,8},{8,13},{9,14},{1... | collective-permute-start | bytes 122888 | tf_op jit(solution)/shard_map/ppermute | solution.py:315
  27.9 1.5 %collective-permute-start.1 = (bf16[144,128]{1,0:T(8,128)(2,1)S(1)}, bf16[144,128]{1,0:T(8,128)(2,1)S(1)}, u32[]{:S(2)}, u32[]{:S(2)}) collective-permute-start(bf16[144,128]{1,0:T(8,128)(2,1)S(1)} %get-tuple-element.24), channel_id=1, source_target_pairs={{0,4},{4,8},{8,12},{12,16},{16,20},{20,24},{24,28},{28,0},{1,5},{5... | collective-permute-start | bytes 110600 | tf_op jit(solution)/shard_map/ppermute | solution.py:314
  29.3 0.3 collective-permute-start
  29.7 2.6 %lower.1 = (f32[24,144,128]{2,1,0:T(8,128)S(1)}, bf16[128,2048]{1,0:T(8,128)(2,1)S(1)}, bf16[128,2048]{1,0:T(8,128)(2,1)S(1)}, bf16[288,2048]{1,0:T(8,128)(2,1)S(1)}) custom-call(bf16[144,2048]{1,0:T(8,128)(2,1)S(1)} %get-tuple-element.16.x_ref, f32[8,2048]{1,0:T(8,128)S(1)} %get-tuple-element.17.info_ref), custom_call_target="tpu_custom_call" | custom-call | tf_op jit(solution)/shard_map/lower/pallas_call | solution.py:326
  32.3 0.3 collective-permute-done.east_ref
  32.6 1.9 %upper.1 = (f32[137,32,128]{2,1,0:T(8,128)}, f32[144,128]{1,0:T(8,128)S(1)}) custom-call(f32[24,144,128]{2,1,0:T(8,128)S(1)} %get-tuple-element.18.acc_ref, bf16[128,2048]{1,0:T(8,128)(2,1)S(1)} %get-tuple-element.19.near_ref, bf16[128,2048]{1,0:T(8,128)(2,1)S(1)} %get-tuple-element.20.far_ref, bf16[288,2048]{1,0:T(8,128)(2,1)S(1)} %get-tuple-element.21.left_ref, ...), custom_call_target="tpu_custom_call" | custom-call | tf_op jit(solution)/shard_map/upper/pallas_call | solution.py:340
  34.5 0.0 collective-permute-done.1.north_ref
  34.5 0.0 collective-permute-done.2.corner_ref
  34.5 0.7 %last.1 = f32[137,32,128]{2,1,0:T(8,128)} custom-call(f32[144,128]{1,0:T(8,128)S(1)} %get-tuple-element.23.south_ref, bf16[144,128]{1,0:T(8,128)(2,1)S(1)} %collective-permute-done.1.north_ref, f32[80,128]{1,0:T(8,128)S(1)} %collective-permute-done.2.corner_ref, f32[137,32,128]{2,1,0:T(8,128)} %get-tuple-element.26.grid_hbm), custom_call_target="tpu_custom_call", output_to_operand_aliasing={{}: (3, {})} | custom-call | tf_op jit(solution)/shard_map/last/pallas_call | solution.py:350
Async XLA Ops:
  27.1 7.4 %collective-permute-start.2 = (f32[80,128]{1,0:T(8,128)S(1)}, f32[80,128]{1,0:T(8,128)S(1)}, u32[]{:S(2)}, u32[]{:S(2)}) collective-permute-start(f32[80,128]{1,0:T(8,128)S(1)} %get-tuple-element.25), channel_id=1, source_target_pairs={{0,5},{1,6},{2,7},{3,4},{4,9},{5,10},{6,11},{7,8},{8,13},{9,14},{1... | collective-permute-start | bytes 122888 | tf_op jit(solution)/shard_map/ppermute | solution.py:315
  27.9 6.7 %collective-permute-start.1 = (bf16[144,128]{1,0:T(8,128)(2,1)S(1)}, bf16[144,128]{1,0:T(8,128)(2,1)S(1)}, u32[]{:S(2)}, u32[]{:S(2)}) collective-permute-start(bf16[144,128]{1,0:T(8,128)(2,1)S(1)} %get-tuple-element.24), channel_id=1, source_target_pairs={{0,4},{4,8},{8,12},{12,16},{16,20},{20,24},{24,28},{28,0},{1,5},{5... | collective-permute-start | bytes 110600 | tf_op jit(solution)/shard_map/ppermute | solution.py:314
  29.3 3.3 %collective-permute-start = (f32[48,128]{1,0:T(8,128)S(1)}, f32[48,128]{1,0:T(8,128)S(1)}, u32[]{:S(2)}, u32[]{:S(2)}) collective-permute-start(f32[48,128]{1,0:T(8,128)S(1)} %get-tuple-element.22), channel_id=1, source_target_pairs={{0,1},{1,2},{2,3},{3,0},{4,5},{5,6},{6,7},{7,4},{8,9},{9,10},{10,1... | collective-permute-start | bytes 73736 | tf_op jit(solution)/shard_map/ppermute | solution.py:324

commit v7 on v6

--- a/solution.py
+++ b/solution.py
@@ -21,6 +21,7 @@
 LOWER = 12
 EDGE_ROWS = -(-(LAT_DEV + 1) // 16) * 16
 FOLD = 3
+OUT_CHUNKS = 4
 PITCH = LANES // FOLD
 JAC_CHUNKS = 2
 
@@ -79,6 +80,7 @@
     for copy in small:
         copy.wait()
     stores = []
+    piece = slots // OUT_CHUNKS
     lane = lane_iota((1, LANES))
     low = lane < cap
     for tile in range(slots // LANES):
@@ -113,9 +115,9 @@
         one, two = swap_halves(whole[:half], whole[half:], cap)
         out_ref[first] = one.astype(BF16)
         out_ref[second] = two.astype(BF16)
-        if (tile + 1) * LANES % chunk == 0:
-            done = tile * LANES // chunk
-            part = pl.ds(done * chunk // cap, chunk // cap)
+        if (tile + 1) * LANES % piece == 0:
+            done = tile * LANES // piece
+            part = pl.ds(done * piece // cap, piece // cap)
             copy = pltpu.make_async_copy(out_ref.at[part], out_hbm.at[part], sems.at[len(small) + JAC_CHUNKS + done])
             copy.start()
             stores.append(copy)
@@ -285,7 +287,7 @@
             pltpu.VMEM((1, slots), F32),
             pltpu.VMEM((2, slots), F32),
             pltpu.VMEM((2, slots), jnp.int32),
-            pltpu.SemaphoreType.DMA((5 + 2 * JAC_CHUNKS,)),
+            pltpu.SemaphoreType.DMA((5 + JAC_CHUNKS + OUT_CHUNKS,)),
         ],
         compiler_params=pltpu.CompilerParams(vmem_limit_bytes=VMEM_ALL),
         name="pack",

time: 35.7 us -> 35.7 us (level)
  no operation moved by 1% of the time
where the time goes in v7:
time: 35.7 us; the launch traced here: 35.2 us
  blocking collectives  24 us (67%)
  Pallas kernels  8.26 us (23%)
  starting transfers between devices  2.53 us (7%)
    all_to_all x1, blocking collectives, per_device(): lax.all_to_all(payload, ('band', 'lon'), split_axis=0, concat_axis=0, til...  24 us
    pallas_call x1, Pallas kernels, per_device(): pl.pallas_call(functools.partial(lower_kernel, levels=levels), out_shape=...  2.59 us
    pallas_call x1, Pallas kernels, per_device(): pl.pallas_call(functools.partial(pack_kernel, cap=cap, lon_count=n_lon),...  2.09 us
    pallas_call x1, Pallas kernels, per_device(): pl.pallas_call(functools.partial(upper_kernel, levels=levels), out_shape=...  1.89 us
    ppermute x1, starting transfers between devices, per_device(): lax.ppermute(north, 'band', [(i, (i + 1) % n_band) for i in bands])  1.48 us
    pallas_call x1, Pallas kernels, per_device(): pl.pallas_call(functools.partial(rim_kernel, cap=cap, levels=levels), out...  0.96 us
    pallas_call x1, Pallas kernels, per_device(): pl.pallas_call(last_kernel, out_shape=struct((levels, LAT_DEV, LON_DEV),...  0.73 us
    ppermute x1, starting transfers between devices, per_device(): lax.ppermute(corner, ('band', 'lon'), [(i * n_lon + j, (i + 1) % n_band *...  0.72 us
  transfers between devices with their start and end apart: 3, of which 1 were waited for; matrix products, arithmetic and copies ran while one was open for 0% of the time, Pallas kernels for 13%

profile of v7, /device:TPU:0, one launch (start us, length us, event | category | flops | bytes accessed | tf_op | source)
XLA Modules:
  0.0 35.2 jit_solution(4959056438721703171)
XLA Ops:
  0.0 2.1 %pack.1 = bf16[32,72,128]{2,1,0:T(8,128)(2,1)} custom-call(s32[1,32]{1,0:T(1,128)} %counts_hbm.1, bf16[137,2048]{1,0:T(8,128)(2,1)} %bitcast.3, f32[1,2048]{1,0:T(1,128)} %bitcast.4, f32[1,2048]{1,0:T(1,128)} %bitcast.5, f32[2,2048]{1,0:T(2,128)} %frac_hbm.1, s32[2,2048]{1,0:T(2,128)} %anchor_hbm.1), custom_call_target="tpu_custom_call" | custom-call | tf_op jit(solution)/shard_map/pack/pallas_call | solution.py:277
  2.1 24.0 %all_to_all.5.recv_ref = bf16[32,72,128]{2,1,0:T(8,128)(2,1)S(1)} all-to-all(bf16[32,72,128]{2,1,0:T(8,128)(2,1)} %pack.1), channel_id=1, replica_groups=mesh['band'=8,'lon'=4] {'band','lon'}, dimensions={0} | all-to-all | bytes 1179648 | tf_op jit(solution)/shard_map/all_to_all | solution.py:296
  26.1 1.0 %rim.1 = (bf16[144,2048]{1,0:T(8,128)(2,1)S(1)}, f32[8,2048]{1,0:T(8,128)S(1)}, f32[48,128]{1,0:T(8,128)S(1)}, bf16[144,128]{1,0:T(8,128)(2,1)S(1)}, f32[80,128]{1,0:T(8,128)S(1)}) custom-call(bf16[32,72,128]{2,1,0:T(8,128)(2,1)S(1)} %all_to_all.5.recv_ref), custom_call_target="tpu_custom_call" | custom-call | tf_op jit(solution)/shard_map/rim/pallas_call | solution.py:299
  27.1 0.7 %collective-permute-start.2 = (f32[80,128]{1,0:T(8,128)S(1)}, f32[80,128]{1,0:T(8,128)S(1)}, u32[]{:S(2)}, u32[]{:S(2)}) collective-permute-start(f32[80,128]{1,0:T(8,128)S(1)} %get-tuple-element.25), channel_id=1, source_target_pairs={{0,5},{1,6},{2,7},{3,4},{4,9},{5,10},{6,11},{7,8},{8,13},{9,14},{1... | collective-permute-start | bytes 122888 | tf_op jit(solution)/shard_map/ppermute | solution.py:317
  27.8 1.5 %collective-permute-start.1 = (bf16[144,128]{1,0:T(8,128)(2,1)S(1)}, bf16[144,128]{1,0:T(8,128)(2,1)S(1)}, u32[]{:S(2)}, u32[]{:S(2)}) collective-permute-start(bf16[144,128]{1,0:T(8,128)(2,1)S(1)} %get-tuple-element.24), channel_id=1, source_target_pairs={{0,4},{4,8},{8,12},{12,16},{16,20},{20,24},{24,28},{28,0},{1,5},{5... | collective-permute-start | bytes 110600 | tf_op jit(solution)/shard_map/ppermute | solution.py:316
  29.3 0.3 collective-permute-start
  29.6 2.6 %lower.1 = (f32[24,144,128]{2,1,0:T(8,128)S(1)}, bf16[128,2048]{1,0:T(8,128)(2,1)S(1)}, bf16[128,2048]{1,0:T(8,128)(2,1)S(1)}, bf16[288,2048]{1,0:T(8,128)(2,1)S(1)}) custom-call(bf16[144,2048]{1,0:T(8,128)(2,1)S(1)} %get-tuple-element.16.x_ref, f32[8,2048]{1,0:T(8,128)S(1)} %get-tuple-element.17.info_ref), custom_call_target="tpu_custom_call" | custom-call | tf_op jit(solution)/shard_map/lower/pallas_call | solution.py:328
  32.2 0.3 collective-permute-done.east_ref
  32.6 1.9 %upper.1 = (f32[137,32,128]{2,1,0:T(8,128)}, f32[144,128]{1,0:T(8,128)S(1)}) custom-call(f32[24,144,128]{2,1,0:T(8,128)S(1)} %get-tuple-element.18.acc_ref, bf16[128,2048]{1,0:T(8,128)(2,1)S(1)} %get-tuple-element.19.near_ref, bf16[128,2048]{1,0:T(8,128)(2,1)S(1)} %get-tuple-element.20.far_ref, bf16[288,2048]{1,0:T(8,128)(2,1)S(1)} %get-tuple-element.21.left_ref, ...), custom_call_target="tpu_custom_call" | custom-call | tf_op jit(solution)/shard_map/upper/pallas_call | solution.py:342
  34.4 0.0 collective-permute-done.1.north_ref
  34.5 0.0 collective-permute-done.2.corner_ref
  34.5 0.7 %last.1 = f32[137,32,128]{2,1,0:T(8,128)} custom-call(f32[144,128]{1,0:T(8,128)S(1)} %get-tuple-element.23.south_ref, bf16[144,128]{1,0:T(8,128)(2,1)S(1)} %collective-permute-done.1.north_ref, f32[80,128]{1,0:T(8,128)S(1)} %collective-permute-done.2.corner_ref, f32[137,32,128]{2,1,0:T(8,128)} %get-tuple-element.26.grid_hbm), custom_call_target="tpu_custom_call", output_to_operand_aliasing={{}: (3, {})} | custom-call | tf_op jit(solution)/shard_map/last/pallas_call | solution.py:352
Async XLA Ops:
  27.1 7.4 %collective-permute-start.2 = (f32[80,128]{1,0:T(8,128)S(1)}, f32[80,128]{1,0:T(8,128)S(1)}, u32[]{:S(2)}, u32[]{:S(2)}) collective-permute-start(f32[80,128]{1,0:T(8,128)S(1)} %get-tuple-element.25), channel_id=1, source_target_pairs={{0,5},{1,6},{2,7},{3,4},{4,9},{5,10},{6,11},{7,8},{8,13},{9,14},{1... | collective-permute-start | bytes 122888 | tf_op jit(solution)/shard_map/ppermute | solution.py:317
  27.8 6.7 %collective-permute-start.1 = (bf16[144,128]{1,0:T(8,128)(2,1)S(1)}, bf16[144,128]{1,0:T(8,128)(2,1)S(1)}, u32[]{:S(2)}, u32[]{:S(2)}) collective-permute-start(bf16[144,128]{1,0:T(8,128)(2,1)S(1)} %get-tuple-element.24), channel_id=1, source_target_pairs={{0,4},{4,8},{8,12},{12,16},{16,20},{20,24},{24,28},{28,0},{1,5},{5... | collective-permute-start | bytes 110600 | tf_op jit(solution)/shard_map/ppermute | solution.py:316
  29.3 3.3 %collective-permute-start = (f32[48,128]{1,0:T(8,128)S(1)}, f32[48,128]{1,0:T(8,128)S(1)}, u32[]{:S(2)}, u32[]{:S(2)}) collective-permute-start(f32[48,128]{1,0:T(8,128)S(1)} %get-tuple-element.22), channel_id=1, source_target_pairs={{0,1},{1,2},{2,3},{3,0},{4,5},{5,6},{6,7},{7,4},{8,9},{9,10},{10,1... | collective-permute-start | bytes 73736 | tf_op jit(solution)/shard_map/ppermute | solution.py:326

commit v8 on v7

--- a/solution.py
+++ b/solution.py
@@ -199,11 +199,11 @@
     far = far_ref[...]
     hot = jnp.concatenate([jnp.where(lat == bf(SPAN * u - 1), far, zero) for u in range(1, GROUPS)], axis=0)
     seam = lax.dot_general(x, hot, NT, preferred_element_type=F32)
-    for first in range(0, LOWER, 2):
-        hot = hot_rows(near_ref, far_ref, within, first, 2)
+    for first in range(0, LOWER, 4):
+        hot = hot_rows(near_ref, far_ref, within, first, 4)
         sums = lax.dot_general(left_ref[...], hot, NT, preferred_element_type=F32)
         for u in range(GROUPS):
-            for i in range(2):
+            for i in range(4):
                 value = sums[u * rows : (u + 1) * rows, i * LON_DEV : (i + 1) * LON_DEV]
                 if first + i == 0 and u > 0:
                     value = value + seam[:, (u - 1) * LON_DEV : u * LON_DEV]

time: 35.7 us -> 35.7 us (level)
  no operation moved by 1% of the time
where the time goes in v8:
time: 35.7 us; the launch traced here: 35.2 us
  blocking collectives  24 us (67%)
  Pallas kernels  8.25 us (23%)
  starting transfers between devices  2.53 us (7%)
    all_to_all x1, blocking collectives, per_device(): lax.all_to_all(payload, ('band', 'lon'), split_axis=0, concat_axis=0, til...  24 us
    pallas_call x1, Pallas kernels, per_device(): pl.pallas_call(functools.partial(lower_kernel, levels=levels), out_shape=...  2.59 us
    pallas_call x1, Pallas kernels, per_device(): pl.pallas_call(functools.partial(pack_kernel, cap=cap, lon_count=n_lon),...  2.09 us
    pallas_call x1, Pallas kernels, per_device(): pl.pallas_call(functools.partial(upper_kernel, levels=levels), out_shape=...  1.89 us
    ppermute x1, starting transfers between devices, per_device(): lax.ppermute(north, 'band', [(i, (i + 1) % n_band) for i in bands])  1.48 us
    pallas_call x1, Pallas kernels, per_device(): pl.pallas_call(functools.partial(rim_kernel, cap=cap, levels=levels), out...  0.96 us
    pallas_call x1, Pallas kernels, per_device(): pl.pallas_call(last_kernel, out_shape=struct((levels, LAT_DEV, LON_DEV),...  0.73 us
    ppermute x1, starting transfers between devices, per_device(): lax.ppermute(corner, ('band', 'lon'), [(i * n_lon + j, (i + 1) % n_band *...  0.72 us
  transfers between devices with their start and end apart: 3, of which 1 were waited for; matrix products, arithmetic and copies ran while one was open for 0% of the time, Pallas kernels for 13%

profile of v8, /device:TPU:0, one launch (start us, length us, event | category | flops | bytes accessed | tf_op | source)
XLA Modules:
  0.0 35.2 jit_solution(9326763782227049709)
XLA Ops:
  0.0 2.1 %pack.1 = bf16[32,72,128]{2,1,0:T(8,128)(2,1)} custom-call(s32[1,32]{1,0:T(1,128)} %counts_hbm.1, bf16[137,2048]{1,0:T(8,128)(2,1)} %bitcast.3, f32[1,2048]{1,0:T(1,128)} %bitcast.4, f32[1,2048]{1,0:T(1,128)} %bitcast.5, f32[2,2048]{1,0:T(2,128)} %frac_hbm.1, s32[2,2048]{1,0:T(2,128)} %anchor_hbm.1), custom_call_target="tpu_custom_call" | custom-call | tf_op jit(solution)/shard_map/pack/pallas_call | solution.py:277
  2.1 24.0 %all_to_all.5.recv_ref = bf16[32,72,128]{2,1,0:T(8,128)(2,1)S(1)} all-to-all(bf16[32,72,128]{2,1,0:T(8,128)(2,1)} %pack.1), channel_id=1, replica_groups=mesh['band'=8,'lon'=4] {'band','lon'}, dimensions={0} | all-to-all | bytes 1179648 | tf_op jit(solution)/shard_map/all_to_all | solution.py:296
  26.1 1.0 %rim.1 = (bf16[144,2048]{1,0:T(8,128)(2,1)S(1)}, f32[8,2048]{1,0:T(8,128)S(1)}, f32[48,128]{1,0:T(8,128)S(1)}, bf16[144,128]{1,0:T(8,128)(2,1)S(1)}, f32[80,128]{1,0:T(8,128)S(1)}) custom-call(bf16[32,72,128]{2,1,0:T(8,128)(2,1)S(1)} %all_to_all.5.recv_ref), custom_call_target="tpu_custom_call" | custom-call | tf_op jit(solution)/shard_map/rim/pallas_call | solution.py:299
  27.1 0.7 %collective-permute-start.2 = (f32[80,128]{1,0:T(8,128)S(1)}, f32[80,128]{1,0:T(8,128)S(1)}, u32[]{:S(2)}, u32[]{:S(2)}) collective-permute-start(f32[80,128]{1,0:T(8,128)S(1)} %get-tuple-element.25), channel_id=1, source_target_pairs={{0,5},{1,6},{2,7},{3,4},{4,9},{5,10},{6,11},{7,8},{8,13},{9,14},{1... | collective-permute-start | bytes 122888 | tf_op jit(solution)/shard_map/ppermute | solution.py:317
  27.8 1.5 %collective-permute-start.1 = (bf16[144,128]{1,0:T(8,128)(2,1)S(1)}, bf16[144,128]{1,0:T(8,128)(2,1)S(1)}, u32[]{:S(2)}, u32[]{:S(2)}) collective-permute-start(bf16[144,128]{1,0:T(8,128)(2,1)S(1)} %get-tuple-element.24), channel_id=1, source_target_pairs={{0,4},{4,8},{8,12},{12,16},{16,20},{20,24},{24,28},{28,0},{1,5},{5... | collective-permute-start | bytes 110600 | tf_op jit(solution)/shard_map/ppermute | solution.py:316
  29.3 0.3 collective-permute-start
  29.6 2.6 %lower.1 = (f32[24,144,128]{2,1,0:T(8,128)S(1)}, bf16[128,2048]{1,0:T(8,128)(2,1)S(1)}, bf16[128,2048]{1,0:T(8,128)(2,1)S(1)}, bf16[288,2048]{1,0:T(8,128)(2,1)S(1)}) custom-call(bf16[144,2048]{1,0:T(8,128)(2,1)S(1)} %get-tuple-element.16.x_ref, f32[8,2048]{1,0:T(8,128)S(1)} %get-tuple-element.17.info_ref), custom_call_target="tpu_custom_call" | custom-call | tf_op jit(solution)/shard_map/lower/pallas_call | solution.py:328
  32.2 0.3 collective-permute-done.east_ref
  32.6 1.9 %upper.1 = (f32[137,32,128]{2,1,0:T(8,128)}, f32[144,128]{1,0:T(8,128)S(1)}) custom-call(f32[24,144,128]{2,1,0:T(8,128)S(1)} %get-tuple-element.18.acc_ref, bf16[128,2048]{1,0:T(8,128)(2,1)S(1)} %get-tuple-element.19.near_ref, bf16[128,2048]{1,0:T(8,128)(2,1)S(1)} %get-tuple-element.20.far_ref, bf16[288,2048]{1,0:T(8,128)(2,1)S(1)} %get-tuple-element.21.left_ref, ...), custom_call_target="tpu_custom_call" | custom-call | tf_op jit(solution)/shard_map/upper/pallas_call | solution.py:342
  34.4 0.0 collective-permute-done.1.north_ref
  34.5 0.0 collective-permute-done.2.corner_ref
  34.5 0.7 %last.1 = f32[137,32,128]{2,1,0:T(8,128)} custom-call(f32[144,128]{1,0:T(8,128)S(1)} %get-tuple-element.23.south_ref, bf16[144,128]{1,0:T(8,128)(2,1)S(1)} %collective-permute-done.1.north_ref, f32[80,128]{1,0:T(8,128)S(1)} %collective-permute-done.2.corner_ref, f32[137,32,128]{2,1,0:T(8,128)} %get-tuple-element.26.grid_hbm), custom_call_target="tpu_custom_call", output_to_operand_aliasing={{}: (3, {})} | custom-call | tf_op jit(solution)/shard_map/last/pallas_call | solution.py:352
Async XLA Ops:
  27.1 7.4 %collective-permute-start.2 = (f32[80,128]{1,0:T(8,128)S(1)}, f32[80,128]{1,0:T(8,128)S(1)}, u32[]{:S(2)}, u32[]{:S(2)}) collective-permute-start(f32[80,128]{1,0:T(8,128)S(1)} %get-tuple-element.25), channel_id=1, source_target_pairs={{0,5},{1,6},{2,7},{3,4},{4,9},{5,10},{6,11},{7,8},{8,13},{9,14},{1... | collective-permute-start | bytes 122888 | tf_op jit(solution)/shard_map/ppermute | solution.py:317
  27.8 6.7 %collective-permute-start.1 = (bf16[144,128]{1,0:T(8,128)(2,1)S(1)}, bf16[144,128]{1,0:T(8,128)(2,1)S(1)}, u32[]{:S(2)}, u32[]{:S(2)}) collective-permute-start(bf16[144,128]{1,0:T(8,128)(2,1)S(1)} %get-tuple-element.24), channel_id=1, source_target_pairs={{0,4},{4,8},{8,12},{12,16},{16,20},{20,24},{24,28},{28,0},{1,5},{5... | collective-permute-start | bytes 110600 | tf_op jit(solution)/shard_map/ppermute | solution.py:316
  29.3 3.3 %collective-permute-start = (f32[48,128]{1,0:T(8,128)S(1)}, f32[48,128]{1,0:T(8,128)S(1)}, u32[]{:S(2)}, u32[]{:S(2)}) collective-permute-start(f32[48,128]{1,0:T(8,128)S(1)} %get-tuple-element.22), channel_id=1, source_target_pairs={{0,1},{1,2},{2,3},{3,0},{4,5},{5,6},{6,7},{7,4},{8,9},{9,10},{10,1... | collective-permute-start | bytes 73736 | tf_op jit(solution)/shard_map/ppermute | solution.py:326
